TPU v7x, 512 devices: a whole 4x8x8 slice. The times are simulated.
512 devices in a mesh: hst: 16 (over z, x_hi), dev: 32 (over y, x_lo, core).
Axes of the slice: x: 4 (x_hi: 2, x_lo: 2; x = x_hi * 2 + x_lo), y: 8, z: 8, core: 2. Of those that a mesh axis runs over, the one named last changes fastest.
Arguments:
- ctx_query: bfloat16 [8192, 8192], P('hst', 'dev'), may hold values from -8 to 8
- ctx_key: bfloat16 [8192, 1024], P(('hst', 'dev')), may hold values from -8 to 8
- ctx_value: bfloat16 [8192, 1024], P(('hst', 'dev')), may hold values from -6 to 6
- query: bfloat16 [1024, 8192], P('hst', 'dev'), may hold values from -8 to 8
- block_lengths: int32 [16], replicated, may hold values from 2 to 512, as said below
- query_positions: int32 [1024], replicated, may hold values from 2 to 8192, as said below
Outputs:
- ctx_out: bfloat16 [8192, 8192], P('hst', 'dev')
- query_out: bfloat16 [1024, 8192], P('hst', 'dev')
Inputs may be any that keep to these rules, and one draw needn't show every extreme that they name: `block_lengths`: the first host block is full, of length 512. `query_positions`: some query token sees the whole context.
All inputs are finite; a program needn't handle non-finite values.
Results may differ from a plain program's by a relative error of at most 0.0039.
Values may be sent and summed in bfloat16 or wider, within the bound.
No kernel may reach another device: no remote copies, remote signals or barrier semaphores. Data moves between devices by JAX's collectives and lax.ppermute only.
A program may use at most 64 MiB of HBM per device.

v0:
```python
import jax
import jax.numpy as jnp
from jax import lax
from jax.sharding import PartitionSpec as P

H = 64
KVH = 8
HD = 128


NEG = -1e30


def spread(shard, axis, root):
    mine = lax.axis_index(axis) == root
    return lax.psum(jnp.where(mine, shard, jnp.zeros_like(shard)), axis)


def combined_all(shard, axis, combine):
    everything = jax.tree.map(lambda part: lax.all_gather(part, axis), shard)
    leading = jax.tree.map(lambda part: part[0], everything)

    def step(k, so_far):
        return combine(so_far, jax.tree.map(lambda part: part[k], everything))

    return lax.fori_loop(1, lax.axis_size(axis), step, leading)


def initial(heads, rows):
    return (
        jnp.full((heads, rows), NEG, jnp.float32),
        jnp.zeros((heads, rows), jnp.float32),
        jnp.zeros((heads, rows, HD), jnp.float32),
    )


def pair_combine(first, second):
    top_value = jnp.maximum(first[0], second[0])
    left_weight = jnp.exp(first[0] - top_value)
    right_weight = jnp.exp(second[0] - top_value)
    sums_new = first[1] * left_weight + second[1] * right_weight
    mixed_new = first[2] * left_weight[..., None] + second[2] * right_weight[..., None]
    return (top_value, sums_new, mixed_new)


def finish(running):
    mixed = running[2] / running[1][..., None]
    heads, rows = running[1].shape
    return jnp.transpose(mixed, (1, 0, 2)).reshape(rows, heads * HD).astype(jnp.bfloat16)


def per_device(ctx_query, ctx_key, ctx_value, query, block_lengths, query_positions):
    dev_count = lax.axis_size("dev")
    host_index = lax.axis_index("hst")
    lane_index = lax.axis_index("dev")
    heads_dev = ctx_query.shape[1] // HD
    block_rows = ctx_key.shape[0] * dev_count
    group_size = H // KVH
    key_column = lane_index * heads_dev // group_size * HD
    host_ids = jnp.arange(block_lengths.shape[0], dtype=jnp.int32)
    own_length = jnp.sum(jnp.where(host_ids == host_index, block_lengths, 0))
    anchor_length = jnp.sum(jnp.where(host_ids == 0, block_lengths, 0))
    ctx_heads = ctx_query.reshape(block_rows, heads_dev, HD)
    query_count = query_positions.shape[0]
    row_ids = jnp.arange(block_rows, dtype=jnp.int32)
    score_scale = HD ** (-0.5)

    def absorb(running, queries, key_slice, value_slice, visible):
        scores = (
            jnp.einsum("rhd,nd->hrn", queries, key_slice, preferred_element_type=jnp.float32)
            * score_scale
        )
        scores = jnp.where(visible[None], scores, NEG)
        maxima = jnp.maximum(running[0], jnp.max(scores, axis=-1))
        weights = jnp.where(visible[None], jnp.exp(scores - maxima[..., None]), 0.0)
        shrink = jnp.exp(running[0] - maxima)
        sums_new = running[1] * shrink + jnp.sum(weights, axis=-1)
        mixed = jnp.einsum(
            "hrn,nd->hrd",
            weights.astype(jnp.bfloat16),
            value_slice,
            preferred_element_type=jnp.float32,
        )
        return (maxima, sums_new, running[2] * shrink[..., None] + mixed)

    def anchor_step(running, key_slice, value_slice, key_index):
        seen = (key_index < anchor_length) & (host_index > 0)
        visible = jnp.broadcast_to(seen[None, :], (block_rows, key_slice.shape[0]))
        return absorb(running, ctx_heads, key_slice, value_slice, visible)

    def local_step(running, key_slice, value_slice, key_index):
        visible = (key_index[None, :] <= row_ids[:, None]) & (key_index[None, :] < own_length)
        return absorb(running, ctx_heads, key_slice, value_slice, visible)

    anchor_key, anchor_value = (spread(ctx_key, "hst", 0), spread(ctx_value, "hst", 0))
    gathered = lax.all_gather(query, "hst", axis=0, tiled=True).reshape(query_count, heads_dev, HD)

    def far_step(running_far, key_slice, value_slice, key_index):
        visible = (key_index[None, :] < own_length) & (
            (host_index * block_rows + key_index)[None, :] < query_positions[:, None]
        )
        return absorb(running_far, gathered, key_slice, value_slice, visible)

    def both_step(states, key_slice, value_slice, key_index):
        return (
            local_step(states[0], key_slice, value_slice, key_index),
            far_step(states[1], key_slice, value_slice, key_index),
        )

    def column_fold(step_fn, state, pieces):
        key_index = jnp.arange(pieces[0].shape[0], dtype=jnp.int32)
        key_slice = lax.dynamic_slice_in_dim(pieces[0], key_column, HD, 1)
        value_slice = lax.dynamic_slice_in_dim(pieces[1], key_column, HD, 1)
        return step_fn(state, key_slice, value_slice, key_index)

    start_ctx = initial(heads_dev, block_rows)
    start_query = initial(heads_dev, query_count)
    running = column_fold(
        anchor_step,
        start_ctx,
        (
            lax.all_gather(anchor_key, "dev", axis=0, tiled=True),
            lax.all_gather(anchor_value, "dev", axis=0, tiled=True),
        ),
    )
    running, partial_value = column_fold(
        both_step,
        (running, start_query),
        (
            lax.all_gather(ctx_key, "dev", axis=0, tiled=True),
            lax.all_gather(ctx_value, "dev", axis=0, tiled=True),
        ),
    )
    ctx_out = finish(running)
    owned = query.shape[0]
    whole = combined_all(partial_value, "hst", pair_combine)
    merged = tuple((lax.dynamic_slice_in_dim(item, host_index * owned, owned, 1) for item in whole))
    return (ctx_out, finish(merged))


def solution(mesh):
    return jax.shard_map(
        per_device,
        mesh=mesh,
        in_specs=(
            P("hst", "dev"),
            P(("hst", "dev"), None),
            P(("hst", "dev"), None),
            P("hst", "dev"),
            P(),
            P(),
        ),
        out_specs=(P("hst", "dev"), P("hst", "dev")),
        check_vma=False,
    )
```

profile of v0, /device:TPU:1, one launch (start us, length us, event | category | flops | bytes accessed | tf_op | source)
XLA Modules:
  0.0 582.3 jit_solution(5461449471693606240)
XLA Ops:
  8.1 1.4 broadcast_select_fusion.1
  9.5 1.4 broadcast_select_fusion
  10.9 0.0 all-gather.13.cloned.1.call-start
  10.9 0.5 all-gather.13.cloned.1.call-update
  11.5 0.5 all-gather.15.cloned.1.call-update
  12.1 152.6 %all-reduce.3.cloned.1.call-done = (bf16[16,1024]{1,0:T(8,128)(2,1)}, bf16[16,1024]{1,0:T(8,128)(2,1)}) async-done(((bf16[16,1024]{1,0:T(8,128)(2,1)}, bf16[16,1024]{1,0:T(8,128)(2,1)}), (bf16[16,1024]{1,0:T(8,128)(2,1)}, bf16[16,1024]{1,0:T(8,128)(2,1)})) %all-reduce.3.cloned.1.call-update) | async-done | bytes 65552 | tf_op jit(solution)/shard_map/psum | solution.py:16
  164.8 1.3 fusion.68
  166.1 32.8 %all_gather.33 = bf16[1024,256]{1,0:T(8,128)(2,1)S(1)} all-gather(bf16[64,256]{1,0:T(8,128)(2,1)} %param.11), channel_id=1, replica_groups=mesh['hst'=16,'dev'=32] {'hst'}, dimensions={0}, use_global_device_ids=true | all-gather | bytes 557056 | tf_op jit(solution)/shard_map/all_gather | solution.py:96
  198.9 0.0 all-gather.17.cloned.1.call-start
  199.0 0.7 iota_compare_fusion.1
  199.6 0.2 copy.36
  199.9 1.1 compare_and_fusion
  201.0 1.9 fusion.3
  202.9 1.1 fusion.5
  204.1 0.8 copy-done.1
  204.9 4.7 fusion.16
  209.7 0.7 fusion.60
  210.3 0.1 fusion.34
  210.5 31.9 %all_gather.35 = f32[16,2,1024]{2,1,0:T(2,128)S(1)} all-gather(f32[1,2,1024]{2,1,0:T(2,128)S(1)} %get-tuple-element.212), channel_id=1, replica_groups=mesh['hst'=16,'dev'=32] {'hst'}, dimensions={0}, use_global_device_ids=true | all-gather | bytes 139264 | tf_op jit(solution)/shard_map/all_gather | solution.py:20
  242.4 30.6 %all-gather.2 = f32[16,2,1024]{2,1,0:T(2,128)S(1)} all-gather(f32[1,2,1024]{2,1,0:T(2,128)S(1)} %get-tuple-element.213), channel_id=2, replica_groups=mesh['hst'=16,'dev'=32] {'hst'}, dimensions={0}, use_global_device_ids=true | all-gather | bytes 139264 | tf_op jit(solution)/shard_map/all_gather | solution.py:20
  273.0 2.8 fusion.11
  275.8 1.5 bitcast_reduce_fusion
  277.3 0.6 fusion.14
  278.0 0.6 fusion.12
  278.5 28.0 %all-gather.11.cloned.1.call-done = bf16[512,1024]{1,0:T(8,128)(2,1)} async-done(((bf16[16,1024]{1,0:T(8,128)(2,1)}), bf16[512,1024]{1,0:T(8,128)(2,1)}) %all-gather.11.cloned.1.call-update) | async-done | bytes 1048592 | tf_op jit(solution)/shard_map/all_gather | solution.py:123
  306.6 1.8 fusion.22
  308.4 1.7 fusion.23
  310.1 0.8 copy.41
  310.9 229.3 %all-gather.17.cloned.1.call-done = f32[32,1024,128]{2,1,0:T(8,128)} async-done(((f32[2,1024,128]{2,1,0:T(8,128)}), f32[32,1024,128]{2,1,0:T(8,128)}) %all-gather.17.cloned.1.call-update) | async-done | bytes 16777232 | tf_op jit(solution)/shard_map/all_gather | solution.py:20
  540.2 1.3 slice.17
  541.5 32.4 %while.19 = (s32[]{:T(128)}, f32[2,1024]{1,0:T(2,128)S(1)}, f32[2,1024]{1,0:T(2,128)S(1)}, f32[2,1024,128]{2,1,0:T(8,128)S(1)}, f32[16,2,1024]{2,1,0:T(2,128)S(1...) while((s32[]{:T(128)}, f32[2,1024]{1,0:T(2,128)S(1)}, ...), condition=%wide.region_11.12_spmd, body=%wide.region_10.11_spmd.sunk | while | flops 798725 | bytes 3227791 | solution.py:26
  541.6 2.1 fusion.89
  543.7 2.1 fusion.89
  545.9 2.1 fusion.89
  548.0 2.1 fusion.89
  550.2 2.1 fusion.89
  552.4 2.1 fusion.89
  554.5 2.1 fusion.89
  556.7 2.1 fusion.89
  558.8 2.1 fusion.89
  561.0 2.1 fusion.89
  563.2 2.1 fusion.89
  565.3 2.1 fusion.89
  567.5 2.1 fusion.89
  569.6 2.1 fusion.89
  571.8 2.1 fusion.89
  573.9 0.1 constant_dynamic-slice_fusion
  574.0 0.7 copy_bitcast_fusion
  (40 shorter events, 1.0 us)
Async XLA Ops:
  8.0 265.0 %copy-start = (bf16[512,256]{1,0:T(8,128)(2,1)S(1)}, bf16[512,256]{1,0:T(8,128)(2,1)}, u32[]{:S(2)}) copy-start(bf16[512,256]{1,0:T(8,128)(2,1)} %param.8) | copy-start | bytes 786436
  8.0 156.7 %all-reduce.3.cloned.1.call-start = ((), (), s32[]{:S(2)}) async-start(), calls=%async_computation.5 | async-start | bytes 131072 | tf_op jit(solution)/shard_map/psum | solution.py:16
  10.9 190.1 %all-gather.13.cloned.1.call-start = ((), (), s32[]{:S(2)}) async-start(), calls=%async_computation.2 | async-start | bytes 1081344 | tf_op jit(solution)/shard_map/all_gather | solution.py:130
  11.5 193.4 %all-gather.15.cloned.1.call-start = ((), (), s32[]{:S(2)}) async-start(), calls=%async_computation.3 | async-start | bytes 1081344 | tf_op jit(solution)/shard_map/all_gather | solution.py:131
  12.1 263.8 %all-gather.9.cloned.1.call-start = ((), (), s32[]{:S(2)}) async-start(), calls=%async_computation | async-start | bytes 1081344 | tf_op jit(solution)/shard_map/all_gather | solution.py:122
  164.7 141.9 %all-gather.11.cloned.1.call-start = ((), (), s32[]{:S(2)}) async-start(), calls=%async_computation.1 | async-start | bytes 1081344 | tf_op jit(solution)/shard_map/all_gather | solution.py:123
  198.9 341.3 %all-gather.17.cloned.1.call-start = ((), (), s32[]{:S(2)}) async-start(), calls=%async_computation.4 | async-start | bytes 17825792 | tf_op jit(solution)/shard_map/all_gather | solution.py:20
  202.9 1.9 copy-start.1
  275.8 2.1 copy-start.2
  306.6 1.8 copy-start.3
Sparse Core Ops, SparseCore 0:
  12.4 152.2 all-reduce.2
Sparse Core Ops, SparseCore 1:
  13.5 70.7 all-gather.12
  86.3 66.3 all-gather.14
  164.8 73.0 all-gather.8
  240.3 66.3 all-gather.10
  310.3 229.9 all-gather.16
where the time goes:
time: 583 us; the launch traced here: 582 us
  waiting for transfers between devices  411 us (70%)
  blocking collectives  95.3 us (16%)
  other arithmetic  41.7 us (7%)
  between operations  15.9 us (3%)
  matrix products  14.4 us (2%)
    all_gather x1, waiting for transfers between devices, combined_all(): everything = jax.tree.map(lambda part: lax.all_gather(part, axis), shard)  229 us
    psum x1, waiting for transfers between devices, spread(): return lax.psum(jnp.where(mine, shard, jnp.zeros_like(shard)), axis)  153 us
    all_gather x2, blocking collectives, combined_all(): everything = jax.tree.map(lambda part: lax.all_gather(part, axis), shard)  62.5 us
    all_gather x1, blocking collectives, per_device(): lax.all_gather(query, 'hst', axis=0, tiled=True)  32.8 us
    add x15, other arithmetic, pair_combine(): first[2] * left_weight[..., None] + second[2] * right_weight[..., None]  31.4 us
    all_gather x1, waiting for transfers between devices, per_device(): lax.all_gather(anchor_value, 'dev', axis=0, tiled=True)  28 us
  transfers between devices with their start and end apart: 6, of which 3 were waited for; matrix products, arithmetic and copies ran while one was open for 4% of the time, Pallas kernels for 0%

commit v1 on v0

v1 whole, which is shorter than its diff:
```python
import math

import jax
import jax.numpy as jnp
from jax import lax
from jax.experimental import pallas as pl
from jax.experimental.pallas import tpu as pltpu
from jax.sharding import PartitionSpec as P

H = 64
KVH = 8
HD = 128
N_Z = 8
N_PAIR = 2
N_LANE = 4
BLK_DEV = 16
QN_DEV = 64
ROWS = 512
SHARE = KVH * BLK_DEV
STAT = 16

NEG = -1e30
FAR = 1 << 20
SCALE2 = HD ** (-0.5) * math.log2(math.e)
BF = jnp.bfloat16
F32 = jnp.float32
NT = (((1,), (1,)), ((), ()))
VMEM_LIMIT = 48 * 1024 * 1024


def call(kernel, out_shape, scratch=(), cost=0):
    return pl.pallas_call(
        kernel,
        out_shape=out_shape,
        scratch_shapes=list(scratch),
        compiler_params=pltpu.CompilerParams(vmem_limit_bytes=VMEM_LIMIT),
        cost_estimate=pl.CostEstimate(
            flops=cost, bytes_accessed=cost // 500, transcendentals=cost // 500
        ),
    )


def pack_kernel(key_ref, value_ref, out_ref):
    for head in range(KVH):
        cols = slice(head * HD, (head + 1) * HD)
        both = jnp.concatenate([key_ref[:, cols], value_ref[:, cols]], axis=1)
        for z in range(N_Z):
            out_ref[z * KVH + head] = both


def with_ones(values):
    return jnp.concatenate([values, jnp.ones_like(values)], axis=1)


def far_kernel(mine_ref, other_ref, kv_ref, pos_ref, len_ref, place_ref, out_ref, q_ref):
    z = place_ref[0]
    pair = place_ref[1]
    lane = place_ref[2]
    q_ref[pair] = mine_ref[...]
    q_ref[1 - pair] = other_ref[...]
    count = kv_ref.shape[0]
    n = lax.broadcasted_iota(jnp.int32, (1, count), 1)
    host = (n // SHARE) * N_PAIR + pair
    inner = ((n % SHARE) // BLK_DEV * N_LANE + lane) * BLK_DEV + n % BLK_DEV
    length = jnp.zeros((1, count), jnp.int32)
    for h in range(N_Z):
        length = jnp.where(n // SHARE == h, len_ref[h * N_PAIR + pair], length)
    spot = jnp.where(inner < length, host * ROWS + inner, FAR).astype(F32)
    limits = jnp.broadcast_to(pos_ref[pl.ds(z, 1), :].astype(F32), (HD, HD)).T
    keys = kv_ref[:, :HD]
    values = with_ones(kv_ref[:, HD:])
    for p in range(N_PAIR):
        lim = limits[p * QN_DEV:(p + 1) * QN_DEV]
        lim = jnp.concatenate([jnp.concatenate([lim] * 4, axis=0)] * (count // HD), axis=1)
        for g in range(0, N_LANE, 2):
            q = q_ref[p, g * QN_DEV:(g + 2) * QN_DEV, :]
            q = jnp.concatenate(
                [q[:QN_DEV, :HD], q[:QN_DEV, HD:], q[QN_DEV:, :HD], q[QN_DEV:, HD:]], axis=0
            )
            s = lax.dot_general(q, keys, NT, preferred_element_type=F32)
            s = jnp.where(spot < lim, s, NEG)
            top = jnp.max(s, axis=1, keepdims=True)
            w = jnp.exp2((s - top) * SCALE2).astype(BF)
            mixed = jnp.dot(w, values, preferred_element_type=F32)
            total = mixed[:, HD:]
            level = top * SCALE2 + jnp.log2(total)
            mean = (mixed[:, :HD] / total).astype(BF)
            for j in range(2):
                d = p * N_LANE + g + j
                base = j * 2 * QN_DEV
                out_ref[d, :QN_DEV, :HD] = mean[base:base + QN_DEV]
                out_ref[d, :QN_DEV, HD:] = mean[base + QN_DEV:base + 2 * QN_DEV]
                flat = level[base:base + 2 * QN_DEV].T[:STAT]
                high = flat.astype(BF)
                rest = flat - high.astype(F32)
                mid = rest.astype(BF)
                low = (rest - mid.astype(F32)).astype(BF)
                row = lax.broadcasted_iota(jnp.int32, (STAT, HD), 0)
                stat = jnp.where(
                    row == 0,
                    high.astype(F32),
                    jnp.where(row == 1, mid.astype(F32), low.astype(F32)),
                )
                out_ref[d, QN_DEV:, :HD] = stat.astype(BF)
                out_ref[d, QN_DEV:, HD:] = jnp.zeros((STAT, HD), BF)


def merge_kernel(in_ref, out_ref):
    parts = in_ref.shape[0]
    levels = []
    for k in range(parts):
        stat = in_ref[k, QN_DEV:, :HD].astype(F32)
        levels.append(stat[0:1] + stat[1:2] + stat[2:3])
    level = jnp.concatenate(levels, axis=0)
    w = jnp.exp2(level - jnp.max(level, axis=0, keepdims=True))
    w = w / jnp.sum(w, axis=0, keepdims=True)
    w = jnp.concatenate([w, jnp.zeros((HD - parts, HD), F32)], axis=0).T
    for h in range(2):
        mixed = jnp.zeros((QN_DEV, HD), F32)
        for k in range(parts):
            column = w[h * QN_DEV:(h + 1) * QN_DEV, k:k + 1]
            mixed += column * in_ref[k, :QN_DEV, h * HD:(h + 1) * HD].astype(F32)
        out_ref[:, h * HD:(h + 1) * HD] = mixed.astype(BF)


def ctx_kernel(q_ref, kv_ref, len_ref, place_ref, out_ref, local_ref):
    host = place_ref[0] * N_PAIR + place_ref[1]
    own = len_ref[host]
    bias = jnp.where(host == 0, jnp.float32(NEG), jnp.float32(0.0))
    for y in range(KVH):
        for g in range(N_LANE):
            to = (y * N_LANE + g) * BLK_DEV
            at = g * 2 * SHARE + y * BLK_DEV
            local_ref[to:to + BLK_DEV, :] = kv_ref[at:at + BLK_DEV, :]
    anchor = jnp.concatenate(
        [kv_ref[g * 2 * SHARE + SHARE:(g + 1) * 2 * SHARE, :] for g in range(N_LANE)], axis=0
    )
    anchor_key, anchor_value = anchor[:, :HD], with_ones(anchor[:, HD:])
    step = 128
    for i in range(ROWS // step):
        n = (i + 1) * step
        rows = slice(i * step, n)
        q = jnp.concatenate([q_ref[rows, :HD], q_ref[rows, HD:]], axis=0)
        a = lax.dot_general(q, anchor_key, NT, preferred_element_type=F32) + bias
        b = lax.dot_general(q, local_ref[:n, :HD], NT, preferred_element_type=F32)
        col = lax.broadcasted_iota(jnp.int32, (2 * step, n), 1)
        row = lax.broadcasted_iota(jnp.int32, (2 * step, n), 0) % step + i * step
        b = jnp.where((col <= row) & (col < own), b, NEG)
        top = jnp.maximum(
            jnp.max(a, axis=1, keepdims=True), jnp.max(b, axis=1, keepdims=True)
        )
        a = jnp.exp2((a - top) * SCALE2).astype(BF)
        b = jnp.exp2((b - top) * SCALE2).astype(BF)
        mixed = jnp.dot(a, anchor_value, preferred_element_type=F32)
        mixed += jnp.dot(b, with_ones(local_ref[:n, HD:]), preferred_element_type=F32)
        mean = (mixed[:, :HD] / mixed[:, HD:]).astype(BF)
        out_ref[rows, :HD] = mean[:step]
        out_ref[rows, HD:] = mean[step:]


def groups(mesh):
    z, x, y, g = range(N_Z), range(N_PAIR), range(KVH), range(N_LANE)
    at = lambda c, d, e, f: (c * N_PAIR + d) * KVH * N_LANE + e * N_LANE + f
    plane = [[at(c, d, e, f) for c in z for e in y] for d in x for f in g]
    line = [[at(c, d, e, f) for d in x for f in g] for c in z for e in y]
    four = [[e * N_LANE + f for f in g] for e in y]
    return plane, line, four


def solution(mesh):
    plane, line, four = groups(mesh)
    both = ("hst", "dev")

    def per_device(ctx_query, ctx_key, ctx_value, query, block_lengths, query_positions):
        host = lax.axis_index("hst")
        z, pair = host // N_PAIR, host % N_PAIR
        place = jnp.stack([z, pair, lax.axis_index("dev") % N_LANE])

        mine = lax.all_gather(query, "dev", axis=0, tiled=True, axis_index_groups=four)
        other = lax.ppermute(mine, "hst", [(i, i ^ 1) for i in range(N_Z * N_PAIR)])

        send = call(pack_kernel, jax.ShapeDtypeStruct((N_Z * KVH, BLK_DEV, 2 * HD), BF))(
            ctx_key, ctx_value
        )
        share = lax.all_to_all(send, both, 0, 0, axis_index_groups=plane)
        share = share.reshape(N_Z * SHARE, 2 * HD)

        first = share[:SHARE]
        passed = lax.ppermute(first, "hst", [(2 * i, 2 * i + 1) for i in range(N_Z)])
        anchor = jnp.where(pair == 0, first, passed)
        local = lax.dynamic_slice_in_dim(share, z * SHARE, SHARE, 0)
        near = lax.all_gather(
            jnp.concatenate([local, anchor], axis=0),
            "dev", axis=0, tiled=True, axis_index_groups=four,
        )

        smem = pl.BlockSpec(memory_space=pltpu.SMEM)
        vmem = pl.BlockSpec(memory_space=pltpu.VMEM)
        params = pltpu.CompilerParams(vmem_limit_bytes=VMEM_LIMIT)
        dests = N_PAIR * N_LANE
        partial = pl.pallas_call(
            far_kernel,
            out_shape=jax.ShapeDtypeStruct((dests, QN_DEV + STAT, 2 * HD), BF),
            in_specs=[vmem, vmem, vmem, vmem, smem, smem],
            out_specs=vmem,
            scratch_shapes=[pltpu.VMEM((N_PAIR, N_LANE * QN_DEV, 2 * HD), BF)],
            compiler_params=params,
            cost_estimate=pl.CostEstimate(
                flops=800_000_000, bytes_accessed=1_200_000, transcendentals=1 << 20
            ),
        )(mine, other, share, query_positions.reshape(N_Z, N_PAIR * QN_DEV), block_lengths, place)
        arrived = lax.all_to_all(partial, both, 0, 0, axis_index_groups=line)

        ctx_out = pl.pallas_call(
            ctx_kernel,
            out_shape=jax.ShapeDtypeStruct(ctx_query.shape, BF),
            in_specs=[vmem, vmem, smem, smem],
            out_specs=vmem,
            scratch_shapes=[pltpu.VMEM((ROWS, 2 * HD), BF)],
            compiler_params=params,
            cost_estimate=pl.CostEstimate(
                flops=800_000_000, bytes_accessed=1_200_000, transcendentals=1 << 20
            ),
        )(ctx_query, near, block_lengths, place)
        query_out = call(merge_kernel, jax.ShapeDtypeStruct(query.shape, BF))(arrived)
        return ctx_out, query_out

    return jax.shard_map(
        per_device,
        mesh=mesh,
        in_specs=(
            P("hst", "dev"),
            P(("hst", "dev"), None),
            P(("hst", "dev"), None),
            P("hst", "dev"),
            P(),
            P(),
        ),
        out_specs=(P("hst", "dev"), P("hst", "dev")),
        check_vma=False,
    )
```

time: 583 us -> 68 us (0.12)
  waiting for transfers between devices: 411 us -> 7.47 us
  blocking collectives: 95.3 us -> 13.9 us
  other arithmetic: 41.7 us -> 0.1 us
  starting transfers between devices: 0.25 us -> 34.5 us
  between operations: 15.9 us -> 0.75 us
  matrix products: 14.4 us -> 0 us
  Pallas kernels: 0 us -> 8.14 us
    all_gather x5 -> x0, waiting for transfers between devices: 257 us -> none  [the longest x1 229 us: combined_all(): everything = jax.tree.map(lambda part: lax.all_gather(part, axis), shard)]
    psum x1 -> x0, waiting for transfers between devices: 153 us -> none  [spread(): return lax.psum(jnp.where(mine, shard, jnp.zeros_like(shard)), axis)]
    all_gather x3 -> x2, blocking collectives: 95.3 us -> 13.9 us  [the longest x1 7.69 us: per_device(): lax.all_gather(jnp.concatenate([local, anchor], axis=0), 'dev', axis=0, t...]
    add x32 -> x0, other arithmetic: 32.1 us -> none  [the longest x15 31.4 us: pair_combine(): first[2] * left_weight[..., None] + second[2] * right_weight[..., None]]
    all_to_all x0 -> x2, starting transfers between devices: none -> 25.1 us  [the longest x1 17.3 us: per_device(): share = lax.all_to_all(send, both, 0, 0, axis_index_groups=plane)]
    dot_general x6 -> x0, matrix products: 14.4 us -> none  [the longest x3 8.21 us: absorb(): jnp.einsum('hrn,nd->hrd', weights.astype(jnp.bfloat16), value_slice, pref...]
    ppermute x0 -> x2, starting transfers between devices: none -> 9.44 us  [the longest x1 4.8 us: per_device(): lax.ppermute(first, 'hst', [(2 * i, 2 * i + 1) for i in range(N_Z)])]
    pallas_call x0 -> x4, Pallas kernels: none -> 8.14 us  [the longest x1 3.18 us: per_device(): pl.pallas_call(far_kernel, out_shape=jax.ShapeDtypeStruct((dests, QN_DEV...]
  transfers between devices with their start and end apart: 6 -> 4, of which waited for: 3 -> 3; matrix products, arithmetic and copies ran while one was open for 4% -> 0% of each run, Pallas kernels for 0% -> 5%
where the time goes in v1:
time: 68 us; the launch traced here: 67.1 us
  starting transfers between devices  34.5 us (51%)
  blocking collectives  13.9 us (20%)
  Pallas kernels  8.14 us (12%)
  waiting for transfers between devices  7.47 us (11%)
  local copies, waits for them, and re-layouts  2.2 us (3%)
  between operations  0.75 us (1%)
    all_to_all x1, starting transfers between devices, per_device(): share = lax.all_to_all(send, both, 0, 0, axis_index_groups=plane)  17.3 us
    all_to_all x1, starting transfers between devices, per_device(): arrived = lax.all_to_all(partial, both, 0, 0, axis_index_groups=line)  7.79 us
    all_gather x1, blocking collectives, per_device(): lax.all_gather(jnp.concatenate([local, anchor], axis=0), 'dev', axis=0, t...  7.69 us
    all_gather x1, blocking collectives, per_device(): lax.all_gather(query, 'dev', axis=0, tiled=True, axis_index_groups=four)  6.21 us
    ppermute x1, starting transfers between devices, per_device(): lax.ppermute(first, 'hst', [(2 * i, 2 * i + 1) for i in range(N_Z)])  4.8 us
    ppermute x1, starting transfers between devices, per_device(): other = lax.ppermute(mine, 'hst', [(i, i ^ 1) for i in range(N_Z * N_PAIR)])  4.64 us
    ppermute x1, waiting for transfers between devices, per_device(): other = lax.ppermute(mine, 'hst', [(i, i ^ 1) for i in range(N_Z * N_PAIR)])  3.56 us
    pallas_call x1, Pallas kernels, per_device(): pl.pallas_call(far_kernel, out_shape=jax.ShapeDtypeStruct((dests, QN_DEV...  3.18 us
  transfers between devices with their start and end apart: 4, of which 3 were waited for; matrix products, arithmetic and copies ran while one was open for 0% of the time, Pallas kernels for 5%

profile of v1, /device:TPU:1, one launch (start us, length us, event | category | flops | bytes accessed | tf_op | source)
XLA Modules:
  0.0 67.1 jit_solution(4334822253120600612)
XLA Ops:
  0.6 0.0 copy-start
  0.6 0.7 %copy-done = bf16[16,1024]{1,0:T(8,128)(2,1)S(1)} copy-done((bf16[16,1024]{1,0:T(8,128)(2,1)S(1)}, bf16[16,1024]{1,0:T(8,128)(2,1)}, u32[]{:S(2)}) %copy-start) | copy-done | bytes 32792
  1.4 0.0 copy-start.1
  1.4 0.8 %copy-done.1 = bf16[16,1024]{1,0:T(8,128)(2,1)S(1)} copy-done((bf16[16,1024]{1,0:T(8,128)(2,1)S(1)}, bf16[16,1024]{1,0:T(8,128)(2,1)}, u32[]{:S(2)}) %copy-start.1) | copy-done | bytes 32792
  2.1 0.8 %shard_map.77 = bf16[64,16,256]{2,1,0:T(8,128)(2,1)} custom-call(bf16[16,1024]{1,0:T(8,128)(2,1)S(1)} %copy-done, bf16[16,1024]{1,0:T(8,128)(2,1)S(1)} %copy-done.1), custom_call_target="tpu_custom_call" | custom-call | tf_op jit(solution)/shard_map/pallas_call | solution.py:182
  3.0 0.0 copy-start.5
  3.0 17.3 %all-to-all-start = ((bf16[64,16,256]{2,1,0:T(8,128)(2,1)}), bf16[64,16,256]{2,1,0:T(8,128)(2,1)S(1)}, u32[]{:S(2)}, u32[]{:S(2)}) async-start(bf16[64,16,256]{2,1,0:T(8,128)(2,1)} %shard_map.77), calls=%async_computation | async-start | bytes 1048576 | tf_op jit(solution)/shard_map/all_to_all | solution.py:185
  20.3 0.0 copy-done.5
  20.3 6.2 %all_gather.7.mine_ref = bf16[256,256]{1,0:T(8,128)(2,1)S(1)} all-gather(bf16[64,256]{1,0:T(8,128)(2,1)S(1)} %copy-done.5), channel_id=1, replica_groups={{0,1,2,3},{4,5,6,7},{8,9,10,11},{12,13,14,15},{16,17,18,19},{20,21,22,2..., dimensions={0}, use_global_device_ids=true | all-gather | bytes 163840 | tf_op jit(solution)/shard_map/all_gather | solution.py:179
  26.5 4.6 %collective-permute-start.1 = (bf16[256,256]{1,0:T(8,128)(2,1)S(1)}, bf16[256,256]{1,0:T(8,128)(2,1)S(1)}, u32[]{:S(2)}, u32[]{:S(2)}) collective-permute-start(bf16[256,256]{1,0:T(8,128)(2,1)S(1)} %all_gather.7.mine_ref), channel_id=1, source_target_pairs={{0,32},{32,0},{64,96},{96,64},{128,160},{160,128},{192,224},{224,1... | collective-permute-start | bytes 393224 | tf_op jit(solution)/shard_map/ppermute | solution.py:180
  31.2 0.0 copy-start.3
  31.2 0.1 pad_add_fusion.place_ref
  31.2 3.6 %collective-permute-done.1.other_ref = bf16[256,256]{1,0:T(8,128)(2,1)S(1)} collective-permute-done((bf16[256,256]{1,0:T(8,128)(2,1)S(1)}, bf16[256,256]{1,0:T(8,128)(2,1)S(1)}, u32[]{:S(2)}, u32[]{:S(2)}) %collective-permute-start.1) | collective-permute-done | bytes 131104 | tf_op jit(solution)/shard_map/ppermute | solution.py:180
  34.8 2.6 %all-to-all-done = bf16[64,16,256]{2,1,0:T(8,128)(2,1)S(1)} async-done(((bf16[64,16,256]{2,1,0:T(8,128)(2,1)}), bf16[64,16,256]{2,1,0:T(8,128)(2,1)S(1)}, u32[]{:S(2)}, u32[]{:S(2)}) %all-to-all-start) | async-done | bytes 524320 | tf_op jit(solution)/shard_map/all_to_all | solution.py:185
  37.4 0.0 copy-start.4
  37.4 0.0 copy-done.3
  37.4 0.7 copy-done.4
  38.1 3.2 %shard_map.79 = bf16[8,80,256]{2,1,0:T(8,128)(2,1)} custom-call(bf16[256,256]{1,0:T(8,128)(2,1)S(1)} %all_gather.7.mine_ref, bf16[256,256]{1,0:T(8,128)(2,1)S(1)} %collective-permute-done.1.other_ref, bf16[1024,256]{1,0:T(8,128)(2,1)S(1)} %bitcast.7, s32[8,128]{1,0:T(8,128)S(1)} %bitcast.9, s32[16]{0:T(128)S(1)} %copy-done.4, s32[3]{0:T(128)S(1)} %pad_add_fusion.place_ref), custom_call_target="tpu_custom_call" | custom-call | flops 800000000 | bytes 1200000 | tf_op jit(solution)/shard_map/pallas_call | solution.py:201
  41.3 7.8 %all-to-all-start.1 = ((bf16[8,80,256]{2,1,0:T(8,128)(2,1)}), bf16[8,80,256]{2,1,0:T(8,128)(2,1)S(1)}, u32[]{:S(2)}, u32[]{:S(2)}) async-start(bf16[8,80,256]{2,1,0:T(8,128)(2,1)} %shard_map.79), calls=%async_computation.1 | async-start | bytes 655360 | tf_op jit(solution)/shard_map/all_to_all | solution.py:212
  49.1 4.8 %collective-permute-start = (bf16[128,256]{1,0:T(8,128)(2,1)S(1)}, bf16[128,256]{1,0:T(8,128)(2,1)S(1)}, u32[]{:S(2)}, u32[]{:S(2)}) collective-permute-start(bf16[128,256]{1,0:T(8,128)(2,1)S(1)} %bitcast.10), channel_id=1, source_target_pairs={{0,32},{64,96},{128,160},{192,224},{256,288},{320,352},{384,416},{... | collective-permute-start | bytes 196616 | tf_op jit(solution)/shard_map/ppermute | solution.py:189
  53.9 1.3 %collective-permute-done = bf16[128,256]{1,0:T(8,128)(2,1)S(1)} collective-permute-done((bf16[128,256]{1,0:T(8,128)(2,1)S(1)}, bf16[128,256]{1,0:T(8,128)(2,1)S(1)}, u32[]{:S(2)}, u32[]{:S(2)}) %collective-permute-start) | collective-permute-done | bytes 65568 | tf_op jit(solution)/shard_map/ppermute | solution.py:189
  55.2 0.0 copy-start.2
  55.2 7.7 %all_gather.6.kv_ref = bf16[1024,256]{1,0:T(8,128)(2,1)S(1)} all-gather(bf16[256,256]{1,0:T(8,128)(2,1)S(1)} %pad_maximum_fusion), channel_id=1, replica_groups={{0,1,2,3},{4,5,6,7},{8,9,10,11},{12,13,14,15},{16,17,18,19},{20,21,22,2..., dimensions={0}, use_global_device_ids=true | all-gather | bytes 655360 | tf_op jit(solution)/shard_map/all_gather | solution.py:192
  62.9 0.0 copy-done.2
  62.9 3.1 %shard_map.78 = bf16[512,256]{1,0:T(8,128)(2,1)} custom-call(bf16[512,256]{1,0:T(8,128)(2,1)S(1)} %copy-done.2, bf16[1024,256]{1,0:T(8,128)(2,1)S(1)} %all_gather.6.kv_ref, s32[16]{0:T(128)S(1)} %copy-done.4, s32[3]{0:T(128)S(1)} %pad_add_fusion.place_ref), custom_call_target="tpu_custom_call" | custom-call | flops 800000000 | bytes 1200000 | tf_op jit(solution)/shard_map/pallas_call | solution.py:214
  66.1 0.0 all-to-all-done.1.in_ref
  66.1 1.0 %shard_map.80 = bf16[64,256]{1,0:T(8,128)(2,1)} custom-call(bf16[8,80,256]{2,1,0:T(8,128)(2,1)S(1)} %all-to-all-done.1.in_ref), custom_call_target="tpu_custom_call" | custom-call | tf_op jit(solution)/shard_map/pallas_call | solution.py:225
  (4 shorter events, 0.0 us)
Async XLA Ops:
  0.6 0.8 %copy-start = (bf16[16,1024]{1,0:T(8,128)(2,1)S(1)}, bf16[16,1024]{1,0:T(8,128)(2,1)}, u32[]{:S(2)}) copy-start(bf16[16,1024]{1,0:T(8,128)(2,1)} %key_ref.1) | copy-start | bytes 98308
  1.4 0.8 %copy-start.1 = (bf16[16,1024]{1,0:T(8,128)(2,1)S(1)}, bf16[16,1024]{1,0:T(8,128)(2,1)}, u32[]{:S(2)}) copy-start(bf16[16,1024]{1,0:T(8,128)(2,1)} %value_ref.1) | copy-start | bytes 98308
  3.0 17.3 %copy-start.5 = (bf16[64,256]{1,0:T(8,128)(2,1)S(1)}, bf16[64,256]{1,0:T(8,128)(2,1)}, u32[]{:S(2)}) copy-start(bf16[64,256]{1,0:T(8,128)(2,1)} %param.9) | copy-start | bytes 98308
  3.0 34.4 %all-to-all-start = ((bf16[64,16,256]{2,1,0:T(8,128)(2,1)}), bf16[64,16,256]{2,1,0:T(8,128)(2,1)S(1)}, u32[]{:S(2)}, u32[]{:S(2)}) async-start(bf16[64,16,256]{2,1,0:T(8,128)(2,1)} %shard_map.77), calls=%async_computation | async-start | bytes 1048576 | tf_op jit(solution)/shard_map/all_to_all | solution.py:185
  26.5 8.3 %collective-permute-start.1 = (bf16[256,256]{1,0:T(8,128)(2,1)S(1)}, bf16[256,256]{1,0:T(8,128)(2,1)S(1)}, u32[]{:S(2)}, u32[]{:S(2)}) collective-permute-start(bf16[256,256]{1,0:T(8,128)(2,1)S(1)} %all_gather.7.mine_ref), channel_id=1, source_target_pairs={{0,32},{32,0},{64,96},{96,64},{128,160},{160,128},{192,224},{224,1... | collective-permute-start | bytes 393224 | tf_op jit(solution)/shard_map/ppermute | solution.py:180
  31.2 6.3 %copy-start.3 = (s32[1024]{0:T(1024)S(1)}, s32[1024]{0:T(1024)}, u32[]{:S(2)}) copy-start(s32[1024]{0:T(1024)} %param.11) | copy-start | bytes 12292
  37.4 0.7 copy-start.4
  41.3 24.8 %all-to-all-start.1 = ((bf16[8,80,256]{2,1,0:T(8,128)(2,1)}), bf16[8,80,256]{2,1,0:T(8,128)(2,1)S(1)}, u32[]{:S(2)}, u32[]{:S(2)}) async-start(bf16[8,80,256]{2,1,0:T(8,128)(2,1)} %shard_map.79), calls=%async_computation.1 | async-start | bytes 655360 | tf_op jit(solution)/shard_map/all_to_all | solution.py:212
  49.1 6.1 %collective-permute-start = (bf16[128,256]{1,0:T(8,128)(2,1)S(1)}, bf16[128,256]{1,0:T(8,128)(2,1)S(1)}, u32[]{:S(2)}, u32[]{:S(2)}) collective-permute-start(bf16[128,256]{1,0:T(8,128)(2,1)S(1)} %bitcast.10), channel_id=1, source_target_pairs={{0,32},{64,96},{128,160},{192,224},{256,288},{320,352},{384,416},{... | collective-permute-start | bytes 196616 | tf_op jit(solution)/shard_map/ppermute | solution.py:189
  55.2 7.7 %copy-start.2 = (bf16[512,256]{1,0:T(8,128)(2,1)S(1)}, bf16[512,256]{1,0:T(8,128)(2,1)}, u32[]{:S(2)}) copy-start(bf16[512,256]{1,0:T(8,128)(2,1)} %q_ref.1) | copy-start | bytes 786436

commit v2 on v1

v2 whole, which is shorter than its diff:
```python
import math

import jax
import jax.numpy as jnp
from jax import lax
from jax.experimental import pallas as pl
from jax.experimental.pallas import tpu as pltpu
from jax.sharding import PartitionSpec as P

H = 64
KVH = 8
HD = 128
N_Z = 8
N_PAIR = 2
N_LANE = 4
BLK_DEV = 16
QN_DEV = 64
ROWS = 512
SHARE = KVH * BLK_DEV
STAT = 16

FAR_ROWS = 256
CTX_ROWS = 128
NEG = -1e30
FAR = 1 << 20
SCALE2 = HD ** (-0.5) * math.log2(math.e)
BF = jnp.bfloat16
F32 = jnp.float32
NT = (((1,), (1,)), ((), ()))
VMEM_LIMIT = 48 * 1024 * 1024


def pack_kernel(key_hbm, value_hbm, out_hbm, key_ref, value_ref, out_ref, sems):
    fetch = [
        pltpu.make_async_copy(key_hbm, key_ref, sems.at[0]),
        pltpu.make_async_copy(value_hbm, value_ref, sems.at[1]),
    ]
    for copy in fetch:
        copy.start()
    for copy in fetch:
        copy.wait()
    for head in range(KVH):
        cols = slice(head * HD, (head + 1) * HD)
        out_ref[head] = jnp.concatenate([key_ref[:, cols], value_ref[:, cols]], axis=1)
    store = [
        pltpu.make_async_copy(out_ref, out_hbm.at[pl.ds(z * KVH, KVH)], sems.at[2 + z])
        for z in range(N_Z)
    ]
    for copy in store:
        copy.start()
    for copy in store:
        copy.wait()


def with_ones(values):
    return jnp.concatenate([values, jnp.ones_like(values)], axis=1)


def prep_kernel(seen_ref, pos_ref, len_ref, place_ref, q_ref, spot_ref, lim_ref, info_ref):
    z = place_ref[0]
    pair = place_ref[1]
    lane = place_ref[2]
    info_ref[0] = z * N_PAIR + pair
    info_ref[1] = len_ref[z * N_PAIR + pair]
    for g in range(N_LANE):
        for p in range(N_PAIR):
            at = (g * N_PAIR + p) * QN_DEV
            for h in range(2):
                rows = slice((2 * g + h) * QN_DEV, (2 * g + h + 1) * QN_DEV)
                q_ref[p, rows] = seen_ref[at:at + QN_DEV, h * HD:(h + 1) * HD]
    n = lax.broadcasted_iota(jnp.int32, spot_ref.shape, 1)
    host = (n // SHARE) * N_PAIR + pair
    inner = ((n % SHARE) // BLK_DEV * N_LANE + lane) * BLK_DEV + n % BLK_DEV
    length = jnp.zeros(spot_ref.shape, jnp.int32)
    for h in range(N_Z):
        length = jnp.where(n // SHARE == h, len_ref[h * N_PAIR + pair], length)
    spot_ref[...] = jnp.where(inner < length, host * ROWS + inner, FAR).astype(F32)
    lim_ref[...] = jnp.broadcast_to(pos_ref[pl.ds(z, 1), :].astype(F32), (HD, HD)).T


def far_kernel(q_ref, kv_ref, spot_ref, lim_ref, out_hbm, out_ref, sems):
    count = kv_ref.shape[0]
    spot = spot_ref[0:1, :]
    keys = kv_ref[:, :HD]
    values = with_ones(kv_ref[:, HD:])
    per = FAR_ROWS // QN_DEV
    blocks = [(p, r) for p in range(N_PAIR) for r in range(0, 2 * N_LANE * QN_DEV, FAR_ROWS)]
    stores = []

    def score(block):
        p, r = block
        return lax.dot_general(
            q_ref[p, r:r + FAR_ROWS], keys, NT, preferred_element_type=F32
        )

    def finish(block, s):
        p, r = block
        lim = lim_ref[p * QN_DEV:(p + 1) * QN_DEV, :]
        lim = jnp.concatenate([jnp.concatenate([lim] * per, axis=0)] * (count // HD), axis=1)
        s = jnp.where(spot < lim, s, NEG)
        top = jnp.max(s, axis=1, keepdims=True)
        w = jnp.exp2((s - top) * SCALE2).astype(BF)
        mixed = jnp.dot(w, values, preferred_element_type=F32)
        total = mixed[:, HD:]
        level = top * SCALE2 + jnp.log2(total)
        mean = (mixed[:, :HD] / total).astype(BF)
        first = p * N_LANE + r // (2 * QN_DEV)
        for j in range(per // 2):
            d = first + j
            base = j * 2 * QN_DEV
            out_ref[d, :QN_DEV, :HD] = mean[base:base + QN_DEV]
            out_ref[d, :QN_DEV, HD:] = mean[base + QN_DEV:base + 2 * QN_DEV]
            flat = level[base:base + 2 * QN_DEV].T[:STAT]
            high = flat.astype(BF).astype(F32)
            rest = flat - high
            mid = rest.astype(BF).astype(F32)
            row = lax.broadcasted_iota(jnp.int32, (STAT, HD), 0)
            stat = jnp.where(row == 0, high, jnp.where(row == 1, mid, rest - mid))
            out_ref[d, QN_DEV:, :HD] = stat.astype(BF)
            out_ref[d, QN_DEV:, HD:] = jnp.zeros((STAT, HD), BF)
        part = pl.ds(first, per // 2)
        copy = pltpu.make_async_copy(out_ref.at[part], out_hbm.at[part], sems.at[len(stores)])
        copy.start()
        stores.append(copy)

    ahead = score(blocks[0])
    for k, block in enumerate(blocks):
        s = ahead
        if k + 1 < len(blocks):
            ahead = score(blocks[k + 1])
        finish(block, s)
    for copy in stores:
        copy.wait()


def merge_kernel(in_ref, out_ref):
    parts = in_ref.shape[0]
    levels = []
    for k in range(parts):
        stat = in_ref[k, QN_DEV:, :HD].astype(F32)
        levels.append(stat[0:1] + stat[1:2] + stat[2:3])
    level = jnp.concatenate(levels, axis=0)
    w = jnp.exp2(level - jnp.max(level, axis=0, keepdims=True))
    w = w / jnp.sum(w, axis=0, keepdims=True)
    w = jnp.concatenate([w, jnp.zeros((HD - parts, HD), F32)], axis=0).T
    for h in range(2):
        mixed = jnp.zeros((QN_DEV, HD), F32)
        for k in range(parts):
            column = w[h * QN_DEV:(h + 1) * QN_DEV, k:k + 1]
            mixed += column * in_ref[k, :QN_DEV, h * HD:(h + 1) * HD].astype(F32)
        out_ref[:, h * HD:(h + 1) * HD] = mixed.astype(BF)


def ctx_kernel(q_ref, kv_ref, info_ref, ctx_hbm, ctx_ref, local_ref, sems):
    alone = info_ref[0] == 0
    own = info_ref[1]
    stores = []
    for y in range(KVH):
        for g in range(N_LANE):
            to = (y * N_LANE + g) * BLK_DEV
            at = (g % 2 * 4 + g // 2) * SHARE + y * BLK_DEV
            local_ref[to:to + BLK_DEV, :] = kv_ref[at:at + BLK_DEV, :]
    anchor = jnp.concatenate(
        [kv_ref[(4 * c + 2) * SHARE:(4 * c + 4) * SHARE, :] for c in range(2)], axis=0
    )
    anchor_key, anchor_value = anchor[:, :HD], with_ones(anchor[:, HD:])
    step = CTX_ROWS
    col = lax.broadcasted_iota(jnp.int32, (1, ROWS), 1)
    spot = jnp.where(col < own, col, FAR)

    def score(i):
        rows = slice(i * step, (i + 1) * step)
        q = jnp.concatenate([q_ref[rows, :HD], q_ref[rows, HD:]], axis=0)
        a = lax.dot_general(q, anchor_key, NT, preferred_element_type=F32)
        b = lax.dot_general(q, local_ref[:(i + 1) * step, :HD], NT, preferred_element_type=F32)
        return a, b

    def finish(i, a, b):
        n = (i + 1) * step
        rows = slice(i * step, n)
        row = lax.broadcasted_iota(jnp.int32, (2 * step, n), 0) % step + i * step
        b = jnp.where(spot[:, :n] <= row, b, NEG)
        top_a = jnp.max(a, axis=1, keepdims=True)
        top = jnp.maximum(jnp.where(alone, NEG, top_a), jnp.max(b, axis=1, keepdims=True))
        a = jnp.exp2((a - jnp.where(alone, -NEG, top)) * SCALE2).astype(BF)
        b = jnp.exp2((b - top) * SCALE2).astype(BF)
        mixed = jnp.dot(a, anchor_value, preferred_element_type=F32)
        mixed += jnp.dot(b, with_ones(local_ref[:n, HD:]), preferred_element_type=F32)
        mean = (mixed[:, :HD] / mixed[:, HD:]).astype(BF)
        ctx_ref[rows, :HD] = mean[:step]
        ctx_ref[rows, HD:] = mean[step:]
        part = pl.ds(i * step, step)
        copy = pltpu.make_async_copy(ctx_ref.at[part], ctx_hbm.at[part], sems.at[i])
        copy.start()
        stores.append(copy)

    count = ROWS // step
    ahead = score(0)
    for i in range(count):
        a, b = ahead
        if i + 1 < count:
            ahead = score(i + 1)
        finish(i, a, b)
    for copy in stores:
        copy.wait()


def groups():
    z, x, y, g = range(N_Z), range(N_PAIR), range(KVH), range(N_LANE)
    at = lambda c, d, e, f: (c * N_PAIR + d) * KVH * N_LANE + e * N_LANE + f
    plane = [[at(c, d, e, f) for c in z for e in y] for d in x for f in g]
    line = [[at(c, d, e, f) for d in x for f in g] for c in z for e in y]
    four = [[e * N_LANE + f for f in g] for e in y]
    side = [[at(c, d, e, 2 * f + k) for d in x for f in range(2)] for c in z for e in y for k in range(2)]
    chip = [[2 * f, 2 * f + 1] for f in range(KVH * N_LANE // 2)]
    pairs = [[2 * c, 2 * c + 1] for c in z]
    return plane, line, four, side, chip, pairs


def solution(mesh):
    plane, line, four, side, chip, pairs = groups()
    both = ("hst", "dev")

    def per_device(ctx_query, ctx_key, ctx_value, query, block_lengths, query_positions):
        host = lax.axis_index("hst")
        z, pair = host // N_PAIR, host % N_PAIR
        smem = pl.BlockSpec(memory_space=pltpu.SMEM)
        vmem = pl.BlockSpec(memory_space=pltpu.VMEM)
        hbm = pl.BlockSpec(memory_space=pltpu.HBM)
        params = pltpu.CompilerParams(vmem_limit_bytes=VMEM_LIMIT)
        heavy = pl.CostEstimate(
            flops=800_000_000, bytes_accessed=1_200_000, transcendentals=1 << 20
        )
        dma = pltpu.SemaphoreType.DMA
        shape = lambda dims, dtype: jax.ShapeDtypeStruct(dims, dtype)

        send = pl.pallas_call(
            pack_kernel,
            out_shape=shape((N_Z * KVH, BLK_DEV, 2 * HD), BF),
            in_specs=[hbm, hbm],
            out_specs=hbm,
            scratch_shapes=[
                pltpu.VMEM(ctx_key.shape, BF),
                pltpu.VMEM(ctx_value.shape, BF),
                pltpu.VMEM((KVH, BLK_DEV, 2 * HD), BF),
                dma((2 + N_Z,)),
            ],
        )(ctx_key, ctx_value)
        share = lax.all_to_all(send, both, 0, 0, axis_index_groups=plane)
        share = share.reshape(N_Z * SHARE, 2 * HD)

        couple = lax.all_gather(query, "hst", axis=0, tiled=True, axis_index_groups=pairs)
        seen = lax.all_gather(couple, "dev", axis=0, tiled=True, axis_index_groups=four)
        place = jnp.stack([z, pair, lax.axis_index("dev") % N_LANE, jnp.zeros_like(z)])
        spans = N_PAIR * QN_DEV
        ask, spot, limits, info = pl.pallas_call(
            prep_kernel,
            out_shape=(
                shape((N_PAIR, 2 * N_LANE * QN_DEV, HD), BF),
                shape((8, N_Z * SHARE), F32),
                shape((spans, spans), F32),
                shape((2,), jnp.int32),
            ),
            in_specs=[vmem, vmem, smem, smem],
            out_specs=(vmem, vmem, vmem, smem),
            compiler_params=params,
        )(seen, query_positions.reshape(N_Z, spans), block_lengths, place)

        share, ask, spot, limits, info = lax.optimization_barrier(
            (share, ask, spot, limits, info)
        )
        local = lax.dynamic_slice_in_dim(share, z * SHARE, SHARE, 0)
        mine = jnp.concatenate([local, share[:SHARE]], axis=0)
        beside = lax.all_to_all(
            jnp.broadcast_to(mine[None], (4, *mine.shape)), both, 0, 0, axis_index_groups=side
        )

        dests = N_PAIR * N_LANE
        piece = (dests, QN_DEV + STAT, 2 * HD)
        partial = pl.pallas_call(
            far_kernel,
            out_shape=shape(piece, BF),
            in_specs=[vmem, vmem, vmem, vmem],
            out_specs=hbm,
            scratch_shapes=[pltpu.VMEM(piece, BF), dma((dests,))],
            compiler_params=params,
            cost_estimate=heavy,
        )(ask, share, spot, limits)
        partial, beside = lax.optimization_barrier((partial, beside))
        half = beside.reshape(N_PAIR, 2, 2 * SHARE, 2 * HD)
        local = lax.dynamic_index_in_dim(half, pair, 0, keepdims=False)[:, :SHARE]
        near = lax.all_gather(
            jnp.stack([local, half[0, :, SHARE:]]).reshape(4 * SHARE, 2 * HD),
            "dev", axis=0, tiled=True, axis_index_groups=chip,
        )
        arrived = lax.all_to_all(partial, both, 0, 0, axis_index_groups=line)

        ctx_out = pl.pallas_call(
            ctx_kernel,
            out_shape=shape(ctx_query.shape, BF),
            in_specs=[vmem, vmem, smem],
            out_specs=hbm,
            scratch_shapes=[
                pltpu.VMEM(ctx_query.shape, BF),
                pltpu.VMEM((ROWS, 2 * HD), BF),
                dma((ROWS // CTX_ROWS,)),
            ],
            compiler_params=params,
            cost_estimate=heavy,
        )(ctx_query, near, info)
        query_out = pl.pallas_call(
            merge_kernel,
            out_shape=shape(query.shape, BF),
            in_specs=[vmem],
            out_specs=vmem,
            compiler_params=params,
        )(arrived)
        return ctx_out, query_out

    return jax.shard_map(
        per_device,
        mesh=mesh,
        in_specs=(
            P("hst", "dev"),
            P(("hst", "dev"), None),
            P(("hst", "dev"), None),
            P("hst", "dev"),
            P(),
            P(),
        ),
        out_specs=(P("hst", "dev"), P("hst", "dev")),
        check_vma=False,
    )
```

time: 68 us -> 65.4 us (0.962)
  starting transfers between devices: 34.5 us -> 29.4 us
  blocking collectives: 13.9 us -> 15 us
  Pallas kernels: 8.14 us -> 9.05 us
  waiting for transfers between devices: 7.47 us -> 8.31 us
    ppermute x2 -> x0, starting transfers between devices: 9.44 us -> none  [the longest x1 4.8 us: per_device(): lax.ppermute(first, 'hst', [(2 * i, 2 * i + 1) for i in range(N_Z)])]
    ppermute x2 -> x0, waiting for transfers between devices: 4.84 us -> none  [the longest x1 3.56 us: per_device(): other = lax.ppermute(mine, 'hst', [(i, i ^ 1) for i in range(N_Z * N_PAIR)])]
    all_to_all x0 -> x1, waiting for transfers between devices: none -> 4.44 us  [per_device(): lax.all_to_all(jnp.broadcast_to(mine[None], (4, *mine.shape)), both, 0, 0...]
    all_to_all x0 -> x1, starting transfers between devices: none -> 4.01 us  [per_device(): lax.all_to_all(jnp.broadcast_to(mine[None], (4, *mine.shape)), both, 0, 0...]
    all_to_all x1, waiting for transfers between devices: 0.01 us -> 2.05 us  [per_device(): arrived = lax.all_to_all(partial, both, 0, 0, axis_index_groups=line)]
    all_gather x2 -> x3, blocking collectives: 13.9 us -> 15 us  [the longest x1 7.42 us: per_device(): lax.all_gather(couple, 'dev', axis=0, tiled=True, axis_index_groups=four)]
    pallas_call x4 -> x5, Pallas kernels: 8.14 us -> 9.05 us  [the longest x1 2.73 us: per_device(): pl.pallas_call(ctx_kernel, out_shape=shape(ctx_query.shape, BF), in_specs...]
    broadcast_in_dim x0 -> x1, local copies, waits for them, and re-layouts: none -> 0.82 us  [per_device(): jnp.broadcast_to(mine[None], (4, *mine.shape))]
  transfers between devices with their start and end apart: 4 -> 3, of which waited for: 3 -> 3; matrix products, arithmetic and copies ran while one was open for 0% -> 0% of each run, Pallas kernels for 5% -> 10%
where the time goes in v2:
time: 65.4 us; the launch traced here: 64.9 us
  starting transfers between devices  29.4 us (45%)
  blocking collectives  15 us (23%)
  Pallas kernels  9.05 us (14%)
  waiting for transfers between devices  8.31 us (13%)
  local copies, waits for them, and re-layouts  2.27 us (3%)
  between operations  0.76 us (1%)
    all_to_all x1, starting transfers between devices, per_device(): share = lax.all_to_all(send, both, 0, 0, axis_index_groups=plane)  17.1 us
    all_to_all x1, starting transfers between devices, per_device(): arrived = lax.all_to_all(partial, both, 0, 0, axis_index_groups=line)  8.27 us
    all_gather x1, blocking collectives, per_device(): lax.all_gather(couple, 'dev', axis=0, tiled=True, axis_index_groups=four)  7.42 us
    all_gather x1, blocking collectives, per_device(): lax.all_gather(query, 'hst', axis=0, tiled=True, axis_index_groups=pairs)  5.23 us
    all_to_all x1, waiting for transfers between devices, per_device(): lax.all_to_all(jnp.broadcast_to(mine[None], (4, *mine.shape)), both, 0, 0...  4.44 us
    all_to_all x1, starting transfers between devices, per_device(): lax.all_to_all(jnp.broadcast_to(mine[None], (4, *mine.shape)), both, 0, 0...  4.01 us
    pallas_call x1, Pallas kernels, per_device(): pl.pallas_call(ctx_kernel, out_shape=shape(ctx_query.shape, BF), in_specs...  2.73 us
    pallas_call x1, Pallas kernels, per_device(): pl.pallas_call(far_kernel, out_shape=shape(piece, BF), in_specs=[vmem, vm...  2.49 us
  transfers between devices with their start and end apart: 3, of which 3 were waited for; matrix products, arithmetic and copies ran while one was open for 0% of the time, Pallas kernels for 10%

profile of v2, /device:TPU:1, one launch (start us, length us, event | category | flops | bytes accessed | tf_op | source)
XLA Modules:
  0.0 64.9 jit_solution(17921454818233877243)
XLA Ops:
  0.6 1.7 %shard_map.77 = bf16[64,16,256]{2,1,0:T(8,128)(2,1)} custom-call(bf16[16,1024]{1,0:T(8,128)(2,1)} %key_hbm.1, bf16[16,1024]{1,0:T(8,128)(2,1)} %value_hbm.1), custom_call_target="tpu_custom_call" | custom-call | tf_op jit(solution)/shard_map/pallas_call | solution.py:237
  2.3 17.1 %all-to-all-start = ((bf16[64,16,256]{2,1,0:T(8,128)(2,1)}), bf16[64,16,256]{2,1,0:T(8,128)(2,1)S(1)}, u32[]{:S(2)}, u32[]{:S(2)}) async-start(bf16[64,16,256]{2,1,0:T(8,128)(2,1)} %shard_map.77), calls=%async_computation | async-start | bytes 1048576 | tf_op jit(solution)/shard_map/all_to_all | solution.py:249
  19.5 0.0 copy-start.3
  19.5 0.7 %copy-done.3 = bf16[64,256]{1,0:T(8,128)(2,1)S(1)} copy-done((bf16[64,256]{1,0:T(8,128)(2,1)S(1)}, bf16[64,256]{1,0:T(8,128)(2,1)}, u32[]{:S(2)}) %copy-start.3) | copy-done | bytes 32792
  20.2 5.2 %all_gather.9 = bf16[128,256]{1,0:T(8,128)(2,1)S(1)} all-gather(bf16[64,256]{1,0:T(8,128)(2,1)S(1)} %copy-done.3), channel_id=1, replica_groups={{0,32},{64,96},{128,160},{192,224},{256,288},{320,352},{384,416},{448,4..., dimensions={0}, use_global_device_ids=true | all-gather | bytes 98304 | tf_op jit(solution)/shard_map/all_gather | solution.py:252
  25.4 7.4 %all_gather.10.seen_ref = bf16[512,256]{1,0:T(8,128)(2,1)S(1)} all-gather(bf16[128,256]{1,0:T(8,128)(2,1)S(1)} %all_gather.9), channel_id=1, replica_groups={{0,1,2,3},{4,5,6,7},{8,9,10,11},{12,13,14,15},{16,17,18,19},{20,21,22,2..., dimensions={0}, use_global_device_ids=true | all-gather | bytes 327680 | tf_op jit(solution)/shard_map/all_gather | solution.py:253
  32.9 0.0 copy-start
  32.9 0.1 pad_add_fusion.place_ref
  32.9 0.0 copy-start.1
  32.9 0.6 copy-done
  33.6 0.0 copy-done.1
  33.6 1.2 %shard_map.78 = (bf16[2,512,128]{2,1,0:T(8,128)(2,1)S(1)}, f32[8,1024]{1,0:T(8,128)S(1)}, f32[128,128]{1,0:T(8,128)S(1)}, s32[2]{0:T(128)S(1)}) custom-call(bf16[512,256]{1,0:T(8,128)(2,1)S(1)} %all_gather.10.seen_ref, s32[8,128]{1,0:T(8,128)S(1)} %bitcast.13, s32[16]{0:T(128)S(1)} %copy-done.1, s32[4]{0:T(128)S(1)} %pad_add_fusion.place_ref), custom_call_target="tpu_custom_call" | custom-call | tf_op jit(solution)/shard_map/pallas_call | solution.py:256
  34.8 1.8 %all-to-all-done = bf16[64,16,256]{2,1,0:T(8,128)(2,1)S(1)} async-done(((bf16[64,16,256]{2,1,0:T(8,128)(2,1)}), bf16[64,16,256]{2,1,0:T(8,128)(2,1)S(1)}, u32[]{:S(2)}, u32[]{:S(2)}) %all-to-all-start) | async-done | bytes 524320 | tf_op jit(solution)/shard_map/all_to_all | solution.py:249
  36.7 0.8 %broadcast_in_dim.2 = bf16[4,256,256]{2,1,0:T(8,128)(2,1)} broadcast(bf16[256,256]{1,0:T(8,128)(2,1)S(1)} %pad_maximum_fusion.1), dimensions={1,2} | broadcast | bytes 655360 | tf_op jit(solution)/shard_map/broadcast_in_dim | solution.py:275
  37.5 4.0 %all-to-all-start.1 = ((bf16[4,256,256]{2,1,0:T(8,128)(2,1)}), bf16[4,256,256]{2,1,0:T(8,128)(2,1)S(1)}, u32[]{:S(2)}, u32[]{:S(2)}) async-start(bf16[4,256,256]{2,1,0:T(8,128)(2,1)} %broadcast_in_dim.2), calls=%async_computation.1 | async-start | bytes 1048576 | tf_op jit(solution)/shard_map/all_to_all | solution.py:274
  41.5 2.5 %shard_map.79 = bf16[8,80,256]{2,1,0:T(8,128)(2,1)} custom-call(bf16[2,512,128]{2,1,0:T(8,128)(2,1)S(1)} %get-tuple-element.17.q_ref, bf16[1024,256]{1,0:T(8,128)(2,1)S(1)} %bitcast.12, f32[8,1024]{1,0:T(8,128)S(1)} %get-tuple-element.19.spot_ref, f32[128,128]{1,0:T(8,128)S(1)} %get-tuple-element.20.lim_ref), custom_call_target="tpu_custom_call" | custom-call | flops 800000000 | bytes 1200000 | tf_op jit(solution)/shard_map/pallas_call | solution.py:280
  44.0 4.4 %all-to-all-done.1 = bf16[4,256,256]{2,1,0:T(8,128)(2,1)S(1)} async-done(((bf16[4,256,256]{2,1,0:T(8,128)(2,1)}), bf16[4,256,256]{2,1,0:T(8,128)(2,1)S(1)}, u32[]{:S(2)}, u32[]{:S(2)}) %all-to-all-start.1) | async-done | bytes 524320 | tf_op jit(solution)/shard_map/all_to_all | solution.py:274
  48.5 8.3 %all-to-all-start.2 = ((bf16[8,80,256]{2,1,0:T(8,128)(2,1)}), bf16[8,80,256]{2,1,0:T(8,128)(2,1)S(1)}, u32[]{:S(2)}, u32[]{:S(2)}) async-start(bf16[8,80,256]{2,1,0:T(8,128)(2,1)} %shard_map.79), calls=%async_computation.2 | async-start | bytes 655360 | tf_op jit(solution)/shard_map/all_to_all | solution.py:296
  56.8 0.0 copy-start.2
  56.8 2.3 %all_gather.11.kv_ref = bf16[1024,256]{1,0:T(8,128)(2,1)S(1)} all-gather(bf16[512,256]{1,0:T(8,128)(2,1)S(1)} %bitcast.16), channel_id=1, replica_groups={{0,1},{2,3},{4,5},{6,7},{8,9},{10,11},{12,13},{14,15},{16,17},{18,19},{..., dimensions={0}, use_global_device_ids=true | all-gather | bytes 786432 | tf_op jit(solution)/shard_map/all_gather | solution.py:292
  59.1 0.0 copy-done.2
  59.1 2.7 %shard_map.80 = bf16[512,256]{1,0:T(8,128)(2,1)} custom-call(bf16[512,256]{1,0:T(8,128)(2,1)S(1)} %copy-done.2, bf16[1024,256]{1,0:T(8,128)(2,1)S(1)} %all_gather.11.kv_ref, s32[2]{0:T(128)S(1)} %get-tuple-element.22.info_ref), custom_call_target="tpu_custom_call" | custom-call | flops 800000000 | bytes 1200000 | tf_op jit(solution)/shard_map/pallas_call | solution.py:298
  61.9 2.0 %all-to-all-done.2.in_ref = bf16[8,80,256]{2,1,0:T(8,128)(2,1)S(1)} async-done(((bf16[8,80,256]{2,1,0:T(8,128)(2,1)}), bf16[8,80,256]{2,1,0:T(8,128)(2,1)S(1)}, u32[]{:S(2)}, u32[]{:S(2)}) %all-to-all-start.2) | async-done | bytes 327712 | tf_op jit(solution)/shard_map/all_to_all | solution.py:296
  63.9 1.0 %shard_map.81 = bf16[64,256]{1,0:T(8,128)(2,1)} custom-call(bf16[8,80,256]{2,1,0:T(8,128)(2,1)S(1)} %all-to-all-done.2.in_ref), custom_call_target="tpu_custom_call" | custom-call | tf_op jit(solution)/shard_map/pallas_call | solution.py:311
  (6 shorter events, 0.1 us)
Async XLA Ops:
  2.3 34.3 %all-to-all-start = ((bf16[64,16,256]{2,1,0:T(8,128)(2,1)}), bf16[64,16,256]{2,1,0:T(8,128)(2,1)S(1)}, u32[]{:S(2)}, u32[]{:S(2)}) async-start(bf16[64,16,256]{2,1,0:T(8,128)(2,1)} %shard_map.77), calls=%async_computation | async-start | bytes 1048576 | tf_op jit(solution)/shard_map/all_to_all | solution.py:249
  19.5 0.8 %copy-start.3 = (bf16[64,256]{1,0:T(8,128)(2,1)S(1)}, bf16[64,256]{1,0:T(8,128)(2,1)}, u32[]{:S(2)}) copy-start(bf16[64,256]{1,0:T(8,128)(2,1)} %param.9) | copy-start | bytes 98308
  32.9 0.7 %copy-start = (s32[1024]{0:T(1024)S(1)}, s32[1024]{0:T(1024)}, u32[]{:S(2)}) copy-start(s32[1024]{0:T(1024)} %param.11) | copy-start | bytes 12292
  32.9 0.7 %copy-start.1 = (s32[16]{0:T(128)S(1)}, s32[16]{0:T(128)}, u32[]{:S(2)}) copy-start(s32[16]{0:T(128)} %len_ref.1) | copy-start | bytes 196
  37.5 10.9 %all-to-all-start.1 = ((bf16[4,256,256]{2,1,0:T(8,128)(2,1)}), bf16[4,256,256]{2,1,0:T(8,128)(2,1)S(1)}, u32[]{:S(2)}, u32[]{:S(2)}) async-start(bf16[4,256,256]{2,1,0:T(8,128)(2,1)} %broadcast_in_dim.2), calls=%async_computation.1 | async-start | bytes 1048576 | tf_op jit(solution)/shard_map/all_to_all | solution.py:274
  48.5 15.4 %all-to-all-start.2 = ((bf16[8,80,256]{2,1,0:T(8,128)(2,1)}), bf16[8,80,256]{2,1,0:T(8,128)(2,1)S(1)}, u32[]{:S(2)}, u32[]{:S(2)}) async-start(bf16[8,80,256]{2,1,0:T(8,128)(2,1)} %shard_map.79), calls=%async_computation.2 | async-start | bytes 655360 | tf_op jit(solution)/shard_map/all_to_all | solution.py:296
  56.8 2.3 %copy-start.2 = (bf16[512,256]{1,0:T(8,128)(2,1)S(1)}, bf16[512,256]{1,0:T(8,128)(2,1)}, u32[]{:S(2)}) copy-start(bf16[512,256]{1,0:T(8,128)(2,1)} %q_ref.1) | copy-start | bytes 786436

commit v3 on v2

--- a/solution.py
+++ b/solution.py
@@ -62,6 +62,7 @@
     lane = place_ref[2]
     info_ref[0] = z * N_PAIR + pair
     info_ref[1] = len_ref[z * N_PAIR + pair]
+    info_ref[2] = lane // 2
     for g in range(N_LANE):
         for p in range(N_PAIR):
             at = (g * N_PAIR + p) * QN_DEV
@@ -158,8 +159,9 @@
     for y in range(KVH):
         for g in range(N_LANE):
             to = (y * N_LANE + g) * BLK_DEV
-            at = (g % 2 * 4 + g // 2) * SHARE + y * BLK_DEV
-            local_ref[to:to + BLK_DEV, :] = kv_ref[at:at + BLK_DEV, :]
+            side = jnp.bitwise_xor(info_ref[2], g // 2)
+            at = pl.multiple_of((g % 2 * 4 + side) * SHARE + y * BLK_DEV, BLK_DEV)
+            local_ref[to:to + BLK_DEV, :] = kv_ref[pl.ds(at, BLK_DEV), :]
     anchor = jnp.concatenate(
         [kv_ref[(4 * c + 2) * SHARE:(4 * c + 4) * SHARE, :] for c in range(2)], axis=0
     )
@@ -259,7 +261,7 @@
                 shape((N_PAIR, 2 * N_LANE * QN_DEV, HD), BF),
                 shape((8, N_Z * SHARE), F32),
                 shape((spans, spans), F32),
-                shape((2,), jnp.int32),
+                shape((3,), jnp.int32),
             ),
             in_specs=[vmem, vmem, smem, smem],
             out_specs=(vmem, vmem, vmem, smem),
@@ -271,8 +273,13 @@
         )
         local = lax.dynamic_slice_in_dim(share, z * SHARE, SHARE, 0)
         mine = jnp.concatenate([local, share[:SHARE]], axis=0)
-        beside = lax.all_to_all(
-            jnp.broadcast_to(mine[None], (4, *mine.shape)), both, 0, 0, axis_index_groups=side
+        hosts, lanes = range(N_Z * N_PAIR), range(KVH * N_LANE)
+        first = share[:SHARE]
+        flip = lax.ppermute(mine, "dev", [(i, i ^ 2) for i in lanes])
+        cross = lax.ppermute(first, "hst", [(i, i + 1) for i in hosts if i % 2 == 0])
+        skew = lax.ppermute(
+            first, both,
+            [(i * len(lanes) + j, (i + 1) * len(lanes) + (j ^ 2)) for i in hosts if i % 2 == 0 for j in lanes],
         )
 
         dests = N_PAIR * N_LANE
@@ -286,11 +293,11 @@
             compiler_params=params,
             cost_estimate=heavy,
         )(ask, share, spot, limits)
-        partial, beside = lax.optimization_barrier((partial, beside))
-        half = beside.reshape(N_PAIR, 2, 2 * SHARE, 2 * HD)
-        local = lax.dynamic_index_in_dim(half, pair, 0, keepdims=False)[:, :SHARE]
+        partial, flip, cross, skew = lax.optimization_barrier((partial, flip, cross, skew))
+        near_anchor = jnp.where(pair == 0, first, cross)
+        far_anchor = jnp.where(pair == 0, flip[SHARE:], skew)
         near = lax.all_gather(
-            jnp.stack([local, half[0, :, SHARE:]]).reshape(4 * SHARE, 2 * HD),
+            jnp.concatenate([local, flip[:SHARE], near_anchor, far_anchor], axis=0),
             "dev", axis=0, tiled=True, axis_index_groups=chip,
         )
         arrived = lax.all_to_all(partial, both, 0, 0, axis_index_groups=line)

time: 65.4 us -> 64.9 us (level)
  starting transfers between devices: 29.4 us -> 34.2 us
  waiting for transfers between devices: 8.31 us -> 3.83 us
  local copies, waits for them, and re-layouts: 2.27 us -> 1.4 us
    ppermute x0 -> x3, starting transfers between devices: none -> 8.77 us  [the longest x1 4.36 us: per_device(): lax.ppermute(first, 'hst', [(i, i + 1) for i in hosts if i % 2 == 0])]
    all_to_all x1 -> x0, waiting for transfers between devices: 4.44 us -> none  [per_device(): lax.all_to_all(jnp.broadcast_to(mine[None], (4, *mine.shape)), both, 0, 0...]
    all_to_all x1 -> x0, starting transfers between devices: 4.01 us -> none  [per_device(): lax.all_to_all(jnp.broadcast_to(mine[None], (4, *mine.shape)), both, 0, 0...]
    broadcast_in_dim x1 -> x0, local copies, waits for them, and re-layouts: 0.82 us -> none  [per_device(): jnp.broadcast_to(mine[None], (4, *mine.shape))]
  transfers between devices with their start and end apart: 3 -> 5, of which waited for: 3 -> 2; matrix products, arithmetic and copies ran while one was open for 0% -> 0% of each run, Pallas kernels for 10% -> 10%
where the time goes in v3:
time: 64.9 us; the launch traced here: 64.4 us
  starting transfers between devices  34.2 us (53%)
  blocking collectives  15 us (23%)
  Pallas kernels  9.05 us (14%)
  waiting for transfers between devices  3.83 us (6%)
  local copies, waits for them, and re-layouts  1.4 us (2%)
  between operations  0.8 us (1%)
    all_to_all x1, starting transfers between devices, per_device(): share = lax.all_to_all(send, both, 0, 0, axis_index_groups=plane)  17.1 us
    all_to_all x1, starting transfers between devices, per_device(): arrived = lax.all_to_all(partial, both, 0, 0, axis_index_groups=line)  8.29 us
    all_gather x1, blocking collectives, per_device(): lax.all_gather(couple, 'dev', axis=0, tiled=True, axis_index_groups=four)  7.42 us
    all_gather x1, blocking collectives, per_device(): lax.all_gather(query, 'hst', axis=0, tiled=True, axis_index_groups=pairs)  5.23 us
    ppermute x1, starting transfers between devices, per_device(): lax.ppermute(first, 'hst', [(i, i + 1) for i in hosts if i % 2 == 0])  4.36 us
    ppermute x1, starting transfers between devices, per_device(): flip = lax.ppermute(mine, 'dev', [(i, i ^ 2) for i in lanes])  3.12 us
    pallas_call x1, Pallas kernels, per_device(): pl.pallas_call(ctx_kernel, out_shape=shape(ctx_query.shape, BF), in_specs...  2.73 us
    pallas_call x1, Pallas kernels, per_device(): pl.pallas_call(far_kernel, out_shape=shape(piece, BF), in_specs=[vmem, vm...  2.47 us
  transfers between devices with their start and end apart: 5, of which 2 were waited for; matrix products, arithmetic and copies ran while one was open for 0% of the time, Pallas kernels for 10%

profile of v3, /device:TPU:1, one launch (start us, length us, event | category | flops | bytes accessed | tf_op | source)
XLA Modules:
  0.0 64.4 jit_solution(16115259508349479840)
XLA Ops:
  0.6 1.7 %shard_map.77 = bf16[64,16,256]{2,1,0:T(8,128)(2,1)} custom-call(bf16[16,1024]{1,0:T(8,128)(2,1)} %key_hbm.1, bf16[16,1024]{1,0:T(8,128)(2,1)} %value_hbm.1), custom_call_target="tpu_custom_call" | custom-call | tf_op jit(solution)/shard_map/pallas_call | solution.py:239
  2.3 17.1 %all-to-all-start = ((bf16[64,16,256]{2,1,0:T(8,128)(2,1)}), bf16[64,16,256]{2,1,0:T(8,128)(2,1)S(1)}, u32[]{:S(2)}, u32[]{:S(2)}) async-start(bf16[64,16,256]{2,1,0:T(8,128)(2,1)} %shard_map.77), calls=%async_computation | async-start | bytes 1048576 | tf_op jit(solution)/shard_map/all_to_all | solution.py:251
  19.5 0.0 copy-start.3
  19.5 0.7 %copy-done.3 = bf16[64,256]{1,0:T(8,128)(2,1)S(1)} copy-done((bf16[64,256]{1,0:T(8,128)(2,1)S(1)}, bf16[64,256]{1,0:T(8,128)(2,1)}, u32[]{:S(2)}) %copy-start.3) | copy-done | bytes 32792
  20.2 5.2 %all_gather.9 = bf16[128,256]{1,0:T(8,128)(2,1)S(1)} all-gather(bf16[64,256]{1,0:T(8,128)(2,1)S(1)} %copy-done.3), channel_id=1, replica_groups={{0,32},{64,96},{128,160},{192,224},{256,288},{320,352},{384,416},{448,4..., dimensions={0}, use_global_device_ids=true | all-gather | bytes 98304 | tf_op jit(solution)/shard_map/all_gather | solution.py:254
  25.5 7.4 %all_gather.10.seen_ref = bf16[512,256]{1,0:T(8,128)(2,1)S(1)} all-gather(bf16[128,256]{1,0:T(8,128)(2,1)S(1)} %all_gather.9), channel_id=1, replica_groups={{0,1,2,3},{4,5,6,7},{8,9,10,11},{12,13,14,15},{16,17,18,19},{20,21,22,2..., dimensions={0}, use_global_device_ids=true | all-gather | bytes 327680 | tf_op jit(solution)/shard_map/all_gather | solution.py:255
  32.9 0.0 copy-start
  32.9 0.1 pad_add_fusion.place_ref
  33.0 0.0 copy-start.1
  33.0 0.6 copy-done
  33.6 0.0 copy-done.1
  33.6 1.2 %shard_map.78 = (bf16[2,512,128]{2,1,0:T(8,128)(2,1)S(1)}, f32[8,1024]{1,0:T(8,128)S(1)}, f32[128,128]{1,0:T(8,128)S(1)}, s32[3]{0:T(128)S(1)}) custom-call(bf16[512,256]{1,0:T(8,128)(2,1)S(1)} %all_gather.10.seen_ref, s32[8,128]{1,0:T(8,128)S(1)} %bitcast.8, s32[16]{0:T(128)S(1)} %copy-done.1, s32[4]{0:T(128)S(1)} %pad_add_fusion.place_ref), custom_call_target="tpu_custom_call" | custom-call | tf_op jit(solution)/shard_map/pallas_call | solution.py:258
  34.8 1.8 %all-to-all-done = bf16[64,16,256]{2,1,0:T(8,128)(2,1)S(1)} async-done(((bf16[64,16,256]{2,1,0:T(8,128)(2,1)}), bf16[64,16,256]{2,1,0:T(8,128)(2,1)S(1)}, u32[]{:S(2)}, u32[]{:S(2)}) %all-to-all-start) | async-done | bytes 524320 | tf_op jit(solution)/shard_map/all_to_all | solution.py:251
  36.7 3.1 %collective-permute-start = (bf16[256,256]{1,0:T(8,128)(2,1)S(1)}, bf16[256,256]{1,0:T(8,128)(2,1)S(1)}, u32[]{:S(2)}, u32[]{:S(2)}) collective-permute-start(bf16[256,256]{1,0:T(8,128)(2,1)S(1)} %pad_maximum_fusion.1), channel_id=1, source_target_pairs={{0,2},{1,3},{2,0},{3,1},{4,6},{5,7},{6,4},{7,5},{8,10},{9,11},{10,... | collective-permute-start | bytes 393224 | tf_op jit(solution)/shard_map/ppermute | solution.py:278
  39.8 4.4 %collective-permute-start.1 = (bf16[128,256]{1,0:T(8,128)(2,1)S(1)}, bf16[128,256]{1,0:T(8,128)(2,1)S(1)}, u32[]{:S(2)}, u32[]{:S(2)}) collective-permute-start(bf16[128,256]{1,0:T(8,128)(2,1)S(1)} %get-tuple-element.29), channel_id=1, source_target_pairs={{0,32},{64,96},{128,160},{192,224},{256,288},{320,352},{384,416},{... | collective-permute-start | bytes 196616 | tf_op jit(solution)/shard_map/ppermute | solution.py:279
  44.2 1.3 %collective-permute-start.2 = (bf16[128,256]{1,0:T(8,128)(2,1)S(1)}, bf16[128,256]{1,0:T(8,128)(2,1)S(1)}, u32[]{:S(2)}, u32[]{:S(2)}) collective-permute-start(bf16[128,256]{1,0:T(8,128)(2,1)S(1)} %get-tuple-element.29), channel_id=1, source_target_pairs={{0,34},{1,35},{2,32},{3,33},{4,38},{5,39},{6,36},{7,37},{8,42},{9,... | collective-permute-start | bytes 196616 | tf_op jit(solution)/shard_map/ppermute | solution.py:280
  45.5 2.5 %shard_map.79 = bf16[8,80,256]{2,1,0:T(8,128)(2,1)} custom-call(bf16[2,512,128]{2,1,0:T(8,128)(2,1)S(1)} %get-tuple-element.20.q_ref, bf16[1024,256]{1,0:T(8,128)(2,1)S(1)} %bitcast.6, f32[8,1024]{1,0:T(8,128)S(1)} %get-tuple-element.21.spot_ref, f32[128,128]{1,0:T(8,128)S(1)} %get-tuple-element.22.lim_ref), custom_call_target="tpu_custom_call" | custom-call | flops 800000000 | bytes 1200000 | tf_op jit(solution)/shard_map/pallas_call | solution.py:287
  47.9 0.0 collective-permute-done.1
  48.0 0.0 collective-permute-done.2
  48.0 0.0 collective-permute-done
  48.0 8.3 %all-to-all-start.1 = ((bf16[8,80,256]{2,1,0:T(8,128)(2,1)}), bf16[8,80,256]{2,1,0:T(8,128)(2,1)S(1)}, u32[]{:S(2)}, u32[]{:S(2)}) async-start(bf16[8,80,256]{2,1,0:T(8,128)(2,1)} %shard_map.79), calls=%async_computation.1 | async-start | bytes 655360 | tf_op jit(solution)/shard_map/all_to_all | solution.py:303
  56.3 0.0 copy-start.2
  56.3 2.3 %all_gather.11.kv_ref = bf16[1024,256]{1,0:T(8,128)(2,1)S(1)} all-gather(bf16[512,256]{1,0:T(8,128)(2,1)S(1)} %pad_maximum_fusion), channel_id=1, replica_groups={{0,1},{2,3},{4,5},{6,7},{8,9},{10,11},{12,13},{14,15},{16,17},{18,19},{..., dimensions={0}, use_global_device_ids=true | all-gather | bytes 786432 | tf_op jit(solution)/shard_map/all_gather | solution.py:299
  58.6 0.0 copy-done.2
  58.6 2.7 %shard_map.80 = bf16[512,256]{1,0:T(8,128)(2,1)} custom-call(bf16[512,256]{1,0:T(8,128)(2,1)S(1)} %copy-done.2, bf16[1024,256]{1,0:T(8,128)(2,1)S(1)} %all_gather.11.kv_ref, s32[3]{0:T(128)S(1)} %get-tuple-element.26.info_ref), custom_call_target="tpu_custom_call" | custom-call | flops 800000000 | bytes 1200000 | tf_op jit(solution)/shard_map/pallas_call | solution.py:305
  61.4 2.0 %all-to-all-done.1.in_ref = bf16[8,80,256]{2,1,0:T(8,128)(2,1)S(1)} async-done(((bf16[8,80,256]{2,1,0:T(8,128)(2,1)}), bf16[8,80,256]{2,1,0:T(8,128)(2,1)S(1)}, u32[]{:S(2)}, u32[]{:S(2)}) %all-to-all-start.1) | async-done | bytes 327712 | tf_op jit(solution)/shard_map/all_to_all | solution.py:303
  63.4 1.0 %shard_map.81 = bf16[64,256]{1,0:T(8,128)(2,1)} custom-call(bf16[8,80,256]{2,1,0:T(8,128)(2,1)S(1)} %all-to-all-done.1.in_ref), custom_call_target="tpu_custom_call" | custom-call | tf_op jit(solution)/shard_map/pallas_call | solution.py:318
  (4 shorter events, 0.1 us)
Async XLA Ops:
  2.3 34.3 %all-to-all-start = ((bf16[64,16,256]{2,1,0:T(8,128)(2,1)}), bf16[64,16,256]{2,1,0:T(8,128)(2,1)S(1)}, u32[]{:S(2)}, u32[]{:S(2)}) async-start(bf16[64,16,256]{2,1,0:T(8,128)(2,1)} %shard_map.77), calls=%async_computation | async-start | bytes 1048576 | tf_op jit(solution)/shard_map/all_to_all | solution.py:251
  19.5 0.8 %copy-start.3 = (bf16[64,256]{1,0:T(8,128)(2,1)S(1)}, bf16[64,256]{1,0:T(8,128)(2,1)}, u32[]{:S(2)}) copy-start(bf16[64,256]{1,0:T(8,128)(2,1)} %param.9) | copy-start | bytes 98308
  32.9 0.7 %copy-start = (s32[1024]{0:T(1024)S(1)}, s32[1024]{0:T(1024)}, u32[]{:S(2)}) copy-start(s32[1024]{0:T(1024)} %param.11) | copy-start | bytes 12292
  33.0 0.7 %copy-start.1 = (s32[16]{0:T(128)S(1)}, s32[16]{0:T(128)}, u32[]{:S(2)}) copy-start(s32[16]{0:T(128)} %len_ref.1) | copy-start | bytes 196
  36.7 11.3 %collective-permute-start = (bf16[256,256]{1,0:T(8,128)(2,1)S(1)}, bf16[256,256]{1,0:T(8,128)(2,1)S(1)}, u32[]{:S(2)}, u32[]{:S(2)}) collective-permute-start(bf16[256,256]{1,0:T(8,128)(2,1)S(1)} %pad_maximum_fusion.1), channel_id=1, source_target_pairs={{0,2},{1,3},{2,0},{3,1},{4,6},{5,7},{6,4},{7,5},{8,10},{9,11},{10,... | collective-permute-start | bytes 393224 | tf_op jit(solution)/shard_map/ppermute | solution.py:278
  39.8 8.1 %collective-permute-start.1 = (bf16[128,256]{1,0:T(8,128)(2,1)S(1)}, bf16[128,256]{1,0:T(8,128)(2,1)S(1)}, u32[]{:S(2)}, u32[]{:S(2)}) collective-permute-start(bf16[128,256]{1,0:T(8,128)(2,1)S(1)} %get-tuple-element.29), channel_id=1, source_target_pairs={{0,32},{64,96},{128,160},{192,224},{256,288},{320,352},{384,416},{... | collective-permute-start | bytes 196616 | tf_op jit(solution)/shard_map/ppermute | solution.py:279
  44.2 3.8 %collective-permute-start.2 = (bf16[128,256]{1,0:T(8,128)(2,1)S(1)}, bf16[128,256]{1,0:T(8,128)(2,1)S(1)}, u32[]{:S(2)}, u32[]{:S(2)}) collective-permute-start(bf16[128,256]{1,0:T(8,128)(2,1)S(1)} %get-tuple-element.29), channel_id=1, source_target_pairs={{0,34},{1,35},{2,32},{3,33},{4,38},{5,39},{6,36},{7,37},{8,42},{9,... | collective-permute-start | bytes 196616 | tf_op jit(solution)/shard_map/ppermute | solution.py:280
  48.0 15.4 %all-to-all-start.1 = ((bf16[8,80,256]{2,1,0:T(8,128)(2,1)}), bf16[8,80,256]{2,1,0:T(8,128)(2,1)S(1)}, u32[]{:S(2)}, u32[]{:S(2)}) async-start(bf16[8,80,256]{2,1,0:T(8,128)(2,1)} %shard_map.79), calls=%async_computation.1 | async-start | bytes 655360 | tf_op jit(solution)/shard_map/all_to_all | solution.py:303
  56.3 2.3 %copy-start.2 = (bf16[512,256]{1,0:T(8,128)(2,1)S(1)}, bf16[512,256]{1,0:T(8,128)(2,1)}, u32[]{:S(2)}) copy-start(bf16[512,256]{1,0:T(8,128)(2,1)} %q_ref.1) | copy-start | bytes 786436

commit v4 on v3

--- a/solution.py
+++ b/solution.py
@@ -276,11 +276,6 @@
         hosts, lanes = range(N_Z * N_PAIR), range(KVH * N_LANE)
         first = share[:SHARE]
         flip = lax.ppermute(mine, "dev", [(i, i ^ 2) for i in lanes])
-        cross = lax.ppermute(first, "hst", [(i, i + 1) for i in hosts if i % 2 == 0])
-        skew = lax.ppermute(
-            first, both,
-            [(i * len(lanes) + j, (i + 1) * len(lanes) + (j ^ 2)) for i in hosts if i % 2 == 0 for j in lanes],
-        )
 
         dests = N_PAIR * N_LANE
         piece = (dests, QN_DEV + STAT, 2 * HD)
@@ -293,7 +288,13 @@
             compiler_params=params,
             cost_estimate=heavy,
         )(ask, share, spot, limits)
-        partial, flip, cross, skew = lax.optimization_barrier((partial, flip, cross, skew))
+        partial, anchor = lax.optimization_barrier((partial, first))
+        cross = lax.ppermute(anchor, "hst", [(i, i + 1) for i in hosts if i % 2 == 0])
+        skew = lax.ppermute(
+            anchor, both,
+            [(i * len(lanes) + j, (i + 1) * len(lanes) + (j ^ 2)) for i in hosts if i % 2 == 0 for j in lanes],
+        )
+        flip, cross, skew = lax.optimization_barrier((flip, cross, skew))
         near_anchor = jnp.where(pair == 0, first, cross)
         far_anchor = jnp.where(pair == 0, flip[SHARE:], skew)
         near = lax.all_gather(

time: 64.9 us -> 64 us (0.986)
  starting transfers between devices: 34.2 us -> 33.3 us
    all_to_all x1, starting transfers between devices: 8.29 us -> 7.41 us  [per_device(): arrived = lax.all_to_all(partial, both, 0, 0, axis_index_groups=line)]
where the time goes in v4:
time: 64 us; the launch traced here: 63.5 us
  starting transfers between devices  33.3 us (52%)
  blocking collectives  15 us (23%)
  Pallas kernels  9.06 us (14%)
  waiting for transfers between devices  3.82 us (6%)
  local copies, waits for them, and re-layouts  1.4 us (2%)
  between operations  0.79 us (1%)
    all_to_all x1, starting transfers between devices, per_device(): share = lax.all_to_all(send, both, 0, 0, axis_index_groups=plane)  17.1 us
    all_gather x1, blocking collectives, per_device(): lax.all_gather(couple, 'dev', axis=0, tiled=True, axis_index_groups=four)  7.42 us
    all_to_all x1, starting transfers between devices, per_device(): arrived = lax.all_to_all(partial, both, 0, 0, axis_index_groups=line)  7.41 us
    all_gather x1, blocking collectives, per_device(): lax.all_gather(query, 'hst', axis=0, tiled=True, axis_index_groups=pairs)  5.23 us
    ppermute x1, starting transfers between devices, per_device(): lax.ppermute(anchor, both, [(i * len(lanes) + j, (i + 1) * len(lanes) + (...  3.72 us
    ppermute x1, starting transfers between devices, per_device(): flip = lax.ppermute(mine, 'dev', [(i, i ^ 2) for i in lanes])  3.12 us
    pallas_call x1, Pallas kernels, per_device(): pl.pallas_call(ctx_kernel, out_shape=shape(ctx_query.shape, BF), in_specs...  2.74 us
    pallas_call x1, Pallas kernels, per_device(): pl.pallas_call(far_kernel, out_shape=shape(piece, BF), in_specs=[vmem, vm...  2.47 us
  transfers between devices with their start and end apart: 5, of which 2 were waited for; matrix products, arithmetic and copies ran while one was open for 0% of the time, Pallas kernels for 10%

profile of v4, /device:TPU:1, one launch (start us, length us, event | category | flops | bytes accessed | tf_op | source)
XLA Modules:
  0.0 63.5 jit_solution(15781381942432123224)
XLA Ops:
  0.6 1.7 %shard_map.77 = bf16[64,16,256]{2,1,0:T(8,128)(2,1)} custom-call(bf16[16,1024]{1,0:T(8,128)(2,1)} %key_hbm.1, bf16[16,1024]{1,0:T(8,128)(2,1)} %value_hbm.1), custom_call_target="tpu_custom_call" | custom-call | tf_op jit(solution)/shard_map/pallas_call | solution.py:239
  2.3 17.1 %all-to-all-start = ((bf16[64,16,256]{2,1,0:T(8,128)(2,1)}), bf16[64,16,256]{2,1,0:T(8,128)(2,1)S(1)}, u32[]{:S(2)}, u32[]{:S(2)}) async-start(bf16[64,16,256]{2,1,0:T(8,128)(2,1)} %shard_map.77), calls=%async_computation | async-start | bytes 1048576 | tf_op jit(solution)/shard_map/all_to_all | solution.py:251
  19.5 0.0 copy-start.3
  19.5 0.7 %copy-done.3 = bf16[64,256]{1,0:T(8,128)(2,1)S(1)} copy-done((bf16[64,256]{1,0:T(8,128)(2,1)S(1)}, bf16[64,256]{1,0:T(8,128)(2,1)}, u32[]{:S(2)}) %copy-start.3) | copy-done | bytes 32792
  20.2 5.2 %all_gather.9 = bf16[128,256]{1,0:T(8,128)(2,1)S(1)} all-gather(bf16[64,256]{1,0:T(8,128)(2,1)S(1)} %copy-done.3), channel_id=1, replica_groups={{0,32},{64,96},{128,160},{192,224},{256,288},{320,352},{384,416},{448,4..., dimensions={0}, use_global_device_ids=true | all-gather | bytes 98304 | tf_op jit(solution)/shard_map/all_gather | solution.py:254
  25.5 7.4 %all_gather.10.seen_ref = bf16[512,256]{1,0:T(8,128)(2,1)S(1)} all-gather(bf16[128,256]{1,0:T(8,128)(2,1)S(1)} %all_gather.9), channel_id=1, replica_groups={{0,1,2,3},{4,5,6,7},{8,9,10,11},{12,13,14,15},{16,17,18,19},{20,21,22,2..., dimensions={0}, use_global_device_ids=true | all-gather | bytes 327680 | tf_op jit(solution)/shard_map/all_gather | solution.py:255
  32.9 0.0 copy-start
  32.9 0.1 pad_add_fusion.place_ref
  33.0 0.0 copy-start.1
  33.0 0.6 copy-done
  33.6 0.0 copy-done.1
  33.6 1.2 %shard_map.78 = (bf16[2,512,128]{2,1,0:T(8,128)(2,1)S(1)}, f32[8,1024]{1,0:T(8,128)S(1)}, f32[128,128]{1,0:T(8,128)S(1)}, s32[3]{0:T(128)S(1)}) custom-call(bf16[512,256]{1,0:T(8,128)(2,1)S(1)} %all_gather.10.seen_ref, s32[8,128]{1,0:T(8,128)S(1)} %bitcast.8, s32[16]{0:T(128)S(1)} %copy-done.1, s32[4]{0:T(128)S(1)} %pad_add_fusion.place_ref), custom_call_target="tpu_custom_call" | custom-call | tf_op jit(solution)/shard_map/pallas_call | solution.py:258
  34.8 1.8 %all-to-all-done = bf16[64,16,256]{2,1,0:T(8,128)(2,1)S(1)} async-done(((bf16[64,16,256]{2,1,0:T(8,128)(2,1)}), bf16[64,16,256]{2,1,0:T(8,128)(2,1)S(1)}, u32[]{:S(2)}, u32[]{:S(2)}) %all-to-all-start) | async-done | bytes 524320 | tf_op jit(solution)/shard_map/all_to_all | solution.py:251
  36.7 3.1 %collective-permute-start = (bf16[256,256]{1,0:T(8,128)(2,1)S(1)}, bf16[256,256]{1,0:T(8,128)(2,1)S(1)}, u32[]{:S(2)}, u32[]{:S(2)}) collective-permute-start(bf16[256,256]{1,0:T(8,128)(2,1)S(1)} %pad_maximum_fusion.1), channel_id=1, source_target_pairs={{0,2},{1,3},{2,0},{3,1},{4,6},{5,7},{6,4},{7,5},{8,10},{9,11},{10,... | collective-permute-start | bytes 393224 | tf_op jit(solution)/shard_map/ppermute | solution.py:278
  39.8 2.5 %shard_map.79 = bf16[8,80,256]{2,1,0:T(8,128)(2,1)} custom-call(bf16[2,512,128]{2,1,0:T(8,128)(2,1)S(1)} %get-tuple-element.21.q_ref, bf16[1024,256]{1,0:T(8,128)(2,1)S(1)} %bitcast.6, f32[8,1024]{1,0:T(8,128)S(1)} %get-tuple-element.22.spot_ref, f32[128,128]{1,0:T(8,128)S(1)} %get-tuple-element.23.lim_ref), custom_call_target="tpu_custom_call" | custom-call | flops 800000000 | bytes 1200000 | tf_op jit(solution)/shard_map/pallas_call | solution.py:282
  42.3 3.7 %collective-permute-start.2 = (bf16[128,256]{1,0:T(8,128)(2,1)S(1)}, bf16[128,256]{1,0:T(8,128)(2,1)S(1)}, u32[]{:S(2)}, u32[]{:S(2)}) collective-permute-start(bf16[128,256]{1,0:T(8,128)(2,1)S(1)} %get-tuple-element.24), channel_id=1, source_target_pairs={{0,34},{1,35},{2,32},{3,33},{4,38},{5,39},{6,36},{7,37},{8,42},{9,... | collective-permute-start | bytes 196616 | tf_op jit(solution)/shard_map/ppermute | solution.py:293
  46.0 1.9 %collective-permute-start.1 = (bf16[128,256]{1,0:T(8,128)(2,1)S(1)}, bf16[128,256]{1,0:T(8,128)(2,1)S(1)}, u32[]{:S(2)}, u32[]{:S(2)}) collective-permute-start(bf16[128,256]{1,0:T(8,128)(2,1)S(1)} %get-tuple-element.24), channel_id=1, source_target_pairs={{0,32},{64,96},{128,160},{192,224},{256,288},{320,352},{384,416},{... | collective-permute-start | bytes 196616 | tf_op jit(solution)/shard_map/ppermute | solution.py:292
  47.9 7.4 %all-to-all-start.1 = ((bf16[8,80,256]{2,1,0:T(8,128)(2,1)}), bf16[8,80,256]{2,1,0:T(8,128)(2,1)S(1)}, u32[]{:S(2)}, u32[]{:S(2)}) async-start(bf16[8,80,256]{2,1,0:T(8,128)(2,1)} %shard_map.79), calls=%async_computation.1 | async-start | bytes 655360 | tf_op jit(solution)/shard_map/all_to_all | solution.py:304
  55.3 0.0 collective-permute-done.2
  55.3 0.0 collective-permute-done.1
  55.4 0.0 collective-permute-done
  55.4 0.0 copy-start.2
  55.4 2.3 %all_gather.11.kv_ref = bf16[1024,256]{1,0:T(8,128)(2,1)S(1)} all-gather(bf16[512,256]{1,0:T(8,128)(2,1)S(1)} %pad_maximum_fusion), channel_id=1, replica_groups={{0,1},{2,3},{4,5},{6,7},{8,9},{10,11},{12,13},{14,15},{16,17},{18,19},{..., dimensions={0}, use_global_device_ids=true | all-gather | bytes 786432 | tf_op jit(solution)/shard_map/all_gather | solution.py:300
  57.7 0.0 copy-done.2
  57.8 2.7 %shard_map.80 = bf16[512,256]{1,0:T(8,128)(2,1)} custom-call(bf16[512,256]{1,0:T(8,128)(2,1)S(1)} %copy-done.2, bf16[1024,256]{1,0:T(8,128)(2,1)S(1)} %all_gather.11.kv_ref, s32[3]{0:T(128)S(1)} %get-tuple-element.28.info_ref), custom_call_target="tpu_custom_call" | custom-call | flops 800000000 | bytes 1200000 | tf_op jit(solution)/shard_map/pallas_call | solution.py:306
  60.5 2.0 %all-to-all-done.1.in_ref = bf16[8,80,256]{2,1,0:T(8,128)(2,1)S(1)} async-done(((bf16[8,80,256]{2,1,0:T(8,128)(2,1)}), bf16[8,80,256]{2,1,0:T(8,128)(2,1)S(1)}, u32[]{:S(2)}, u32[]{:S(2)}) %all-to-all-start.1) | async-done | bytes 327712 | tf_op jit(solution)/shard_map/all_to_all | solution.py:304
  62.5 1.0 %shard_map.81 = bf16[64,256]{1,0:T(8,128)(2,1)} custom-call(bf16[8,80,256]{2,1,0:T(8,128)(2,1)S(1)} %all-to-all-done.1.in_ref), custom_call_target="tpu_custom_call" | custom-call | tf_op jit(solution)/shard_map/pallas_call | solution.py:319
  (4 shorter events, 0.1 us)
Async XLA Ops:
  2.3 34.3 %all-to-all-start = ((bf16[64,16,256]{2,1,0:T(8,128)(2,1)}), bf16[64,16,256]{2,1,0:T(8,128)(2,1)S(1)}, u32[]{:S(2)}, u32[]{:S(2)}) async-start(bf16[64,16,256]{2,1,0:T(8,128)(2,1)} %shard_map.77), calls=%async_computation | async-start | bytes 1048576 | tf_op jit(solution)/shard_map/all_to_all | solution.py:251
  19.5 0.8 %copy-start.3 = (bf16[64,256]{1,0:T(8,128)(2,1)S(1)}, bf16[64,256]{1,0:T(8,128)(2,1)}, u32[]{:S(2)}) copy-start(bf16[64,256]{1,0:T(8,128)(2,1)} %param.9) | copy-start | bytes 98308
  32.9 0.7 %copy-start = (s32[1024]{0:T(1024)S(1)}, s32[1024]{0:T(1024)}, u32[]{:S(2)}) copy-start(s32[1024]{0:T(1024)} %param.11) | copy-start | bytes 12292
  33.0 0.7 %copy-start.1 = (s32[16]{0:T(128)S(1)}, s32[16]{0:T(128)}, u32[]{:S(2)}) copy-start(s32[16]{0:T(128)} %len_ref.1) | copy-start | bytes 196
  36.7 18.7 %collective-permute-start = (bf16[256,256]{1,0:T(8,128)(2,1)S(1)}, bf16[256,256]{1,0:T(8,128)(2,1)S(1)}, u32[]{:S(2)}, u32[]{:S(2)}) collective-permute-start(bf16[256,256]{1,0:T(8,128)(2,1)S(1)} %pad_maximum_fusion.1), channel_id=1, source_target_pairs={{0,2},{1,3},{2,0},{3,1},{4,6},{5,7},{6,4},{7,5},{8,10},{9,11},{10,... | collective-permute-start | bytes 393224 | tf_op jit(solution)/shard_map/ppermute | solution.py:278
  42.3 13.1 %collective-permute-start.2 = (bf16[128,256]{1,0:T(8,128)(2,1)S(1)}, bf16[128,256]{1,0:T(8,128)(2,1)S(1)}, u32[]{:S(2)}, u32[]{:S(2)}) collective-permute-start(bf16[128,256]{1,0:T(8,128)(2,1)S(1)} %get-tuple-element.24), channel_id=1, source_target_pairs={{0,34},{1,35},{2,32},{3,33},{4,38},{5,39},{6,36},{7,37},{8,42},{9,... | collective-permute-start | bytes 196616 | tf_op jit(solution)/shard_map/ppermute | solution.py:293
  46.0 9.3 %collective-permute-start.1 = (bf16[128,256]{1,0:T(8,128)(2,1)S(1)}, bf16[128,256]{1,0:T(8,128)(2,1)S(1)}, u32[]{:S(2)}, u32[]{:S(2)}) collective-permute-start(bf16[128,256]{1,0:T(8,128)(2,1)S(1)} %get-tuple-element.24), channel_id=1, source_target_pairs={{0,32},{64,96},{128,160},{192,224},{256,288},{320,352},{384,416},{... | collective-permute-start | bytes 196616 | tf_op jit(solution)/shard_map/ppermute | solution.py:292
  47.9 14.5 %all-to-all-start.1 = ((bf16[8,80,256]{2,1,0:T(8,128)(2,1)}), bf16[8,80,256]{2,1,0:T(8,128)(2,1)S(1)}, u32[]{:S(2)}, u32[]{:S(2)}) async-start(bf16[8,80,256]{2,1,0:T(8,128)(2,1)} %shard_map.79), calls=%async_computation.1 | async-start | bytes 655360 | tf_op jit(solution)/shard_map/all_to_all | solution.py:304
  55.4 2.3 %copy-start.2 = (bf16[512,256]{1,0:T(8,128)(2,1)S(1)}, bf16[512,256]{1,0:T(8,128)(2,1)}, u32[]{:S(2)}) copy-start(bf16[512,256]{1,0:T(8,128)(2,1)} %q_ref.1) | copy-start | bytes 786436

commit v5 on v4

--- a/solution.py
+++ b/solution.py
@@ -19,7 +19,7 @@
 SHARE = KVH * BLK_DEV
 STAT = 16
 
-FAR_ROWS = 256
+FAR_BLOCKS = ((0, 0, 128), (0, 128, 256), (0, 384, 128), (1, 0, 256), (1, 256, 128), (1, 384, 128))
 CTX_ROWS = 128
 NEG = -1e30
 FAR = 1 << 20
@@ -56,13 +56,14 @@
     return jnp.concatenate([values, jnp.ones_like(values)], axis=1)
 
 
-def prep_kernel(seen_ref, pos_ref, len_ref, place_ref, q_ref, spot_ref, lim_ref, info_ref):
+def prep_kernel(seen_ref, pos_ref, len_ref, place_ref, q_ref, spot_ref, lim_ref, own_ref, gate_ref):
     z = place_ref[0]
     pair = place_ref[1]
     lane = place_ref[2]
-    info_ref[0] = z * N_PAIR + pair
-    info_ref[1] = len_ref[z * N_PAIR + pair]
-    info_ref[2] = lane // 2
+    here = z * N_PAIR + pair
+    col = lax.broadcasted_iota(jnp.int32, own_ref.shape, 1)
+    own_ref[...] = jnp.where(col < len_ref[here], col, FAR).astype(F32)
+    gate_ref[...] = jnp.full(gate_ref.shape, jnp.where(here == 0, -NEG, 0.0), F32)
     for g in range(N_LANE):
         for p in range(N_PAIR):
             at = (g * N_PAIR + p) * QN_DEV
@@ -84,18 +85,18 @@
     spot = spot_ref[0:1, :]
     keys = kv_ref[:, :HD]
     values = with_ones(kv_ref[:, HD:])
-    per = FAR_ROWS // QN_DEV
-    blocks = [(p, r) for p in range(N_PAIR) for r in range(0, 2 * N_LANE * QN_DEV, FAR_ROWS)]
+    blocks = FAR_BLOCKS
     stores = []
 
     def score(block):
-        p, r = block
+        p, r, size = block
         return lax.dot_general(
-            q_ref[p, r:r + FAR_ROWS], keys, NT, preferred_element_type=F32
+            q_ref[p, r:r + size], keys, NT, preferred_element_type=F32
         )
 
     def finish(block, s):
-        p, r = block
+        p, r, size = block
+        per = size // QN_DEV
         lim = lim_ref[p * QN_DEV:(p + 1) * QN_DEV, :]
         lim = jnp.concatenate([jnp.concatenate([lim] * per, axis=0)] * (count // HD), axis=1)
         s = jnp.where(spot < lim, s, NEG)
@@ -152,23 +153,20 @@
         out_ref[:, h * HD:(h + 1) * HD] = mixed.astype(BF)
 
 
-def ctx_kernel(q_ref, kv_ref, info_ref, ctx_hbm, ctx_ref, local_ref, sems):
-    alone = info_ref[0] == 0
-    own = info_ref[1]
+def ctx_kernel(q_ref, kv_ref, own_ref, gate_ref, ctx_hbm, ctx_ref, local_ref, sems):
+    gate = gate_ref[0:1, 0:1]
     stores = []
     for y in range(KVH):
         for g in range(N_LANE):
             to = (y * N_LANE + g) * BLK_DEV
-            side = jnp.bitwise_xor(info_ref[2], g // 2)
-            at = pl.multiple_of((g % 2 * 4 + side) * SHARE + y * BLK_DEV, BLK_DEV)
-            local_ref[to:to + BLK_DEV, :] = kv_ref[pl.ds(at, BLK_DEV), :]
+            at = (g % 2 * 4 + g // 2) * SHARE + y * BLK_DEV
+            local_ref[to:to + BLK_DEV, :] = kv_ref[at:at + BLK_DEV, :]
     anchor = jnp.concatenate(
         [kv_ref[(4 * c + 2) * SHARE:(4 * c + 4) * SHARE, :] for c in range(2)], axis=0
     )
     anchor_key, anchor_value = anchor[:, :HD], with_ones(anchor[:, HD:])
     step = CTX_ROWS
-    col = lax.broadcasted_iota(jnp.int32, (1, ROWS), 1)
-    spot = jnp.where(col < own, col, FAR)
+    spot = own_ref[0:1, :]
 
     def score(i):
         rows = slice(i * step, (i + 1) * step)
@@ -180,11 +178,11 @@
     def finish(i, a, b):
         n = (i + 1) * step
         rows = slice(i * step, n)
-        row = lax.broadcasted_iota(jnp.int32, (2 * step, n), 0) % step + i * step
+        row = (lax.broadcasted_iota(jnp.int32, (2 * step, n), 0) % step + i * step).astype(F32)
         b = jnp.where(spot[:, :n] <= row, b, NEG)
         top_a = jnp.max(a, axis=1, keepdims=True)
-        top = jnp.maximum(jnp.where(alone, NEG, top_a), jnp.max(b, axis=1, keepdims=True))
-        a = jnp.exp2((a - jnp.where(alone, -NEG, top)) * SCALE2).astype(BF)
+        top = jnp.maximum(top_a - gate, jnp.max(b, axis=1, keepdims=True))
+        a = jnp.exp2((a - (top + gate)) * SCALE2).astype(BF)
         b = jnp.exp2((b - top) * SCALE2).astype(BF)
         mixed = jnp.dot(a, anchor_value, preferred_element_type=F32)
         mixed += jnp.dot(b, with_ones(local_ref[:n, HD:]), preferred_element_type=F32)
@@ -197,11 +195,11 @@
         stores.append(copy)
 
     count = ROWS // step
-    ahead = score(0)
-    for i in range(count):
+    ahead = score(count - 1)
+    for i in reversed(range(count)):
         a, b = ahead
-        if i + 1 < count:
-            ahead = score(i + 1)
+        if i > 0:
+            ahead = score(i - 1)
         finish(i, a, b)
     for copy in stores:
         copy.wait()
@@ -255,21 +253,22 @@
         seen = lax.all_gather(couple, "dev", axis=0, tiled=True, axis_index_groups=four)
         place = jnp.stack([z, pair, lax.axis_index("dev") % N_LANE, jnp.zeros_like(z)])
         spans = N_PAIR * QN_DEV
-        ask, spot, limits, info = pl.pallas_call(
+        ask, spot, limits, own_spot, gate = pl.pallas_call(
             prep_kernel,
             out_shape=(
                 shape((N_PAIR, 2 * N_LANE * QN_DEV, HD), BF),
                 shape((8, N_Z * SHARE), F32),
                 shape((spans, spans), F32),
-                shape((3,), jnp.int32),
+                shape((8, ROWS), F32),
+                shape((8, HD), F32),
             ),
             in_specs=[vmem, vmem, smem, smem],
-            out_specs=(vmem, vmem, vmem, smem),
+            out_specs=(vmem,) * 5,
             compiler_params=params,
         )(seen, query_positions.reshape(N_Z, spans), block_lengths, place)
 
-        share, ask, spot, limits, info = lax.optimization_barrier(
-            (share, ask, spot, limits, info)
+        share, ask, spot, limits, own_spot, gate = lax.optimization_barrier(
+            (share, ask, spot, limits, own_spot, gate)
         )
         local = lax.dynamic_slice_in_dim(share, z * SHARE, SHARE, 0)
         mine = jnp.concatenate([local, share[:SHARE]], axis=0)
@@ -297,8 +296,18 @@
         flip, cross, skew = lax.optimization_barrier((flip, cross, skew))
         near_anchor = jnp.where(pair == 0, first, cross)
         far_anchor = jnp.where(pair == 0, flip[SHARE:], skew)
+        even = lax.axis_index("dev") % N_LANE < 2
+        other = flip[:SHARE]
         near = lax.all_gather(
-            jnp.concatenate([local, flip[:SHARE], near_anchor, far_anchor], axis=0),
+            jnp.concatenate(
+                [
+                    jnp.where(even, local, other),
+                    jnp.where(even, other, local),
+                    near_anchor,
+                    far_anchor,
+                ],
+                axis=0,
+            ),
             "dev", axis=0, tiled=True, axis_index_groups=chip,
         )
         arrived = lax.all_to_all(partial, both, 0, 0, axis_index_groups=line)
@@ -306,7 +315,7 @@
         ctx_out = pl.pallas_call(
             ctx_kernel,
             out_shape=shape(ctx_query.shape, BF),
-            in_specs=[vmem, vmem, smem],
+            in_specs=[vmem] * 4,
             out_specs=hbm,
             scratch_shapes=[
                 pltpu.VMEM(ctx_query.shape, BF),
@@ -315,7 +324,7 @@
             ],
             compiler_params=params,
             cost_estimate=heavy,
-        )(ctx_query, near, info)
+        )(ctx_query, near, own_spot, gate)
         query_out = pl.pallas_call(
             merge_kernel,
             out_shape=shape(query.shape, BF),

time: 64 us -> 64 us (level)
  Pallas kernels: 9.06 us -> 8.25 us
  waiting for transfers between devices: 3.82 us -> 4.63 us
  transfers between devices with their start and end apart: 5 -> 5, of which waited for: 2 -> 2; matrix products, arithmetic and copies ran while one was open for 0% -> 0% of each run, Pallas kernels for 10% -> 9%
where the time goes in v5:
time: 64 us; the launch traced here: 63.5 us
  starting transfers between devices  33.3 us (52%)
  blocking collectives  15 us (23%)
  Pallas kernels  8.25 us (13%)
  waiting for transfers between devices  4.63 us (7%)
  local copies, waits for them, and re-layouts  1.4 us (2%)
  between operations  0.8 us (1%)
    all_to_all x1, starting transfers between devices, per_device(): share = lax.all_to_all(send, both, 0, 0, axis_index_groups=plane)  17.1 us
    all_gather x1, blocking collectives, per_device(): lax.all_gather(couple, 'dev', axis=0, tiled=True, axis_index_groups=four)  7.42 us
    all_to_all x1, starting transfers between devices, per_device(): arrived = lax.all_to_all(partial, both, 0, 0, axis_index_groups=line)  7.4 us
    all_gather x1, blocking collectives, per_device(): lax.all_gather(query, 'hst', axis=0, tiled=True, axis_index_groups=pairs)  5.23 us
    ppermute x1, starting transfers between devices, per_device(): lax.ppermute(anchor, both, [(i * len(lanes) + j, (i + 1) * len(lanes) + (...  3.72 us
    ppermute x1, starting transfers between devices, per_device(): flip = lax.ppermute(mine, 'dev', [(i, i ^ 2) for i in lanes])  3.12 us
    pallas_call x1, Pallas kernels, per_device(): pl.pallas_call(far_kernel, out_shape=shape(piece, BF), in_specs=[vmem, vm...  2.48 us
    pallas_call x1, Pallas kernels, per_device(): pl.pallas_call(ctx_kernel, out_shape=shape(ctx_query.shape, BF), in_specs...  2.41 us
  transfers between devices with their start and end apart: 5, of which 2 were waited for; matrix products, arithmetic and copies ran while one was open for 0% of the time, Pallas kernels for 9%

profile of v5, /device:TPU:1, one launch (start us, length us, event | category | flops | bytes accessed | tf_op | source)
XLA Modules:
  0.0 63.5 jit_solution(7276586972853977935)
XLA Ops:
  0.6 1.7 %shard_map.77 = bf16[64,16,256]{2,1,0:T(8,128)(2,1)} custom-call(bf16[16,1024]{1,0:T(8,128)(2,1)} %key_hbm.1, bf16[16,1024]{1,0:T(8,128)(2,1)} %value_hbm.1), custom_call_target="tpu_custom_call" | custom-call | tf_op jit(solution)/shard_map/pallas_call | solution.py:237
  2.3 17.1 %all-to-all-start = ((bf16[64,16,256]{2,1,0:T(8,128)(2,1)}), bf16[64,16,256]{2,1,0:T(8,128)(2,1)S(1)}, u32[]{:S(2)}, u32[]{:S(2)}) async-start(bf16[64,16,256]{2,1,0:T(8,128)(2,1)} %shard_map.77), calls=%async_computation | async-start | bytes 1048576 | tf_op jit(solution)/shard_map/all_to_all | solution.py:249
  19.5 0.0 copy-start.3
  19.5 0.7 %copy-done.3 = bf16[64,256]{1,0:T(8,128)(2,1)S(1)} copy-done((bf16[64,256]{1,0:T(8,128)(2,1)S(1)}, bf16[64,256]{1,0:T(8,128)(2,1)}, u32[]{:S(2)}) %copy-start.3) | copy-done | bytes 32792
  20.2 5.2 %all_gather.9 = bf16[128,256]{1,0:T(8,128)(2,1)S(1)} all-gather(bf16[64,256]{1,0:T(8,128)(2,1)S(1)} %copy-done.3), channel_id=1, replica_groups={{0,32},{64,96},{128,160},{192,224},{256,288},{320,352},{384,416},{448,4..., dimensions={0}, use_global_device_ids=true | all-gather | bytes 98304 | tf_op jit(solution)/shard_map/all_gather | solution.py:252
  25.5 7.4 %all_gather.10.seen_ref = bf16[512,256]{1,0:T(8,128)(2,1)S(1)} all-gather(bf16[128,256]{1,0:T(8,128)(2,1)S(1)} %all_gather.9), channel_id=1, replica_groups={{0,1,2,3},{4,5,6,7},{8,9,10,11},{12,13,14,15},{16,17,18,19},{20,21,22,2..., dimensions={0}, use_global_device_ids=true | all-gather | bytes 327680 | tf_op jit(solution)/shard_map/all_gather | solution.py:253
  32.9 0.0 copy-start
  32.9 0.1 pad_add_fusion.place_ref
  33.0 0.0 copy-start.1
  33.0 0.6 copy-done
  33.6 0.0 copy-done.1
  33.6 0.7 %shard_map.78 = (bf16[2,512,128]{2,1,0:T(8,128)(2,1)S(1)}, f32[8,1024]{1,0:T(8,128)S(1)}, f32[128,128]{1,0:T(8,128)S(1)}, f32[8,512]{1,0:T(8,128)S(1)}, f32[8,128]{1,0:T(8,128)S(1)}) custom-call(bf16[512,256]{1,0:T(8,128)(2,1)S(1)} %all_gather.10.seen_ref, s32[8,128]{1,0:T(8,128)S(1)} %bitcast.8, s32[16]{0:T(128)S(1)} %copy-done.1, s32[4]{0:T(128)S(1)} %pad_add_fusion.place_ref), custom_call_target="tpu_custom_call" | custom-call | tf_op jit(solution)/shard_map/pallas_call | solution.py:256
  34.3 2.3 %all-to-all-done = bf16[64,16,256]{2,1,0:T(8,128)(2,1)S(1)} async-done(((bf16[64,16,256]{2,1,0:T(8,128)(2,1)}), bf16[64,16,256]{2,1,0:T(8,128)(2,1)S(1)}, u32[]{:S(2)}, u32[]{:S(2)}) %all-to-all-start) | async-done | bytes 524320 | tf_op jit(solution)/shard_map/all_to_all | solution.py:249
  36.7 3.1 %collective-permute-start = (bf16[256,256]{1,0:T(8,128)(2,1)S(1)}, bf16[256,256]{1,0:T(8,128)(2,1)S(1)}, u32[]{:S(2)}, u32[]{:S(2)}) collective-permute-start(bf16[256,256]{1,0:T(8,128)(2,1)S(1)} %pad_maximum_fusion.1), channel_id=1, source_target_pairs={{0,2},{1,3},{2,0},{3,1},{4,6},{5,7},{6,4},{7,5},{8,10},{9,11},{10,... | collective-permute-start | bytes 393224 | tf_op jit(solution)/shard_map/ppermute | solution.py:277
  39.8 2.5 %shard_map.79 = bf16[8,80,256]{2,1,0:T(8,128)(2,1)} custom-call(bf16[2,512,128]{2,1,0:T(8,128)(2,1)S(1)} %get-tuple-element.24.q_ref, bf16[1024,256]{1,0:T(8,128)(2,1)S(1)} %bitcast.6, f32[8,1024]{1,0:T(8,128)S(1)} %get-tuple-element.25.spot_ref, f32[128,128]{1,0:T(8,128)S(1)} %get-tuple-element.26.lim_ref), custom_call_target="tpu_custom_call" | custom-call | flops 800000000 | bytes 1200000 | tf_op jit(solution)/shard_map/pallas_call | solution.py:281
  42.3 3.7 %collective-permute-start.2 = (bf16[128,256]{1,0:T(8,128)(2,1)S(1)}, bf16[128,256]{1,0:T(8,128)(2,1)S(1)}, u32[]{:S(2)}, u32[]{:S(2)}) collective-permute-start(bf16[128,256]{1,0:T(8,128)(2,1)S(1)} %get-tuple-element.27), channel_id=1, source_target_pairs={{0,34},{1,35},{2,32},{3,33},{4,38},{5,39},{6,36},{7,37},{8,42},{9,... | collective-permute-start | bytes 196616 | tf_op jit(solution)/shard_map/ppermute | solution.py:292
  46.0 1.9 %collective-permute-start.1 = (bf16[128,256]{1,0:T(8,128)(2,1)S(1)}, bf16[128,256]{1,0:T(8,128)(2,1)S(1)}, u32[]{:S(2)}, u32[]{:S(2)}) collective-permute-start(bf16[128,256]{1,0:T(8,128)(2,1)S(1)} %get-tuple-element.27), channel_id=1, source_target_pairs={{0,32},{64,96},{128,160},{192,224},{256,288},{320,352},{384,416},{... | collective-permute-start | bytes 196616 | tf_op jit(solution)/shard_map/ppermute | solution.py:291
  48.0 7.4 %all-to-all-start.1 = ((bf16[8,80,256]{2,1,0:T(8,128)(2,1)}), bf16[8,80,256]{2,1,0:T(8,128)(2,1)S(1)}, u32[]{:S(2)}, u32[]{:S(2)}) async-start(bf16[8,80,256]{2,1,0:T(8,128)(2,1)} %shard_map.79), calls=%async_computation.1 | async-start | bytes 655360 | tf_op jit(solution)/shard_map/all_to_all | solution.py:313
  55.4 0.0 collective-permute-done.2
  55.4 0.0 collective-permute-done.1
  55.4 0.0 collective-permute-done
  55.4 0.0 copy-start.2
  55.5 2.3 %all_gather.11.kv_ref = bf16[1024,256]{1,0:T(8,128)(2,1)S(1)} all-gather(bf16[512,256]{1,0:T(8,128)(2,1)S(1)} %pad_maximum_fusion), channel_id=1, replica_groups={{0,1},{2,3},{4,5},{6,7},{8,9},{10,11},{12,13},{14,15},{16,17},{18,19},{..., dimensions={0}, use_global_device_ids=true | all-gather | bytes 786432 | tf_op jit(solution)/shard_map/all_gather | solution.py:301
  57.8 0.0 copy-done.2
  57.8 2.4 %shard_map.80 = bf16[512,256]{1,0:T(8,128)(2,1)} custom-call(bf16[512,256]{1,0:T(8,128)(2,1)S(1)} %copy-done.2, bf16[1024,256]{1,0:T(8,128)(2,1)S(1)} %all_gather.11.kv_ref, f32[8,512]{1,0:T(8,128)S(1)} %get-tuple-element.31.own_ref, f32[8,128]{1,0:T(8,128)S(1)} %get-tuple-element.32.gate_ref), custom_call_target="tpu_custom_call" | custom-call | flops 800000000 | bytes 1200000 | tf_op jit(solution)/shard_map/pallas_call | solution.py:315
  60.2 2.3 %all-to-all-done.1.in_ref = bf16[8,80,256]{2,1,0:T(8,128)(2,1)S(1)} async-done(((bf16[8,80,256]{2,1,0:T(8,128)(2,1)}), bf16[8,80,256]{2,1,0:T(8,128)(2,1)S(1)}, u32[]{:S(2)}, u32[]{:S(2)}) %all-to-all-start.1) | async-done | bytes 327712 | tf_op jit(solution)/shard_map/all_to_all | solution.py:313
  62.5 1.0 %shard_map.81 = bf16[64,256]{1,0:T(8,128)(2,1)} custom-call(bf16[8,80,256]{2,1,0:T(8,128)(2,1)S(1)} %all-to-all-done.1.in_ref), custom_call_target="tpu_custom_call" | custom-call | tf_op jit(solution)/shard_map/pallas_call | solution.py:328
  (4 shorter events, 0.1 us)
Async XLA Ops:
  2.3 34.3 %all-to-all-start = ((bf16[64,16,256]{2,1,0:T(8,128)(2,1)}), bf16[64,16,256]{2,1,0:T(8,128)(2,1)S(1)}, u32[]{:S(2)}, u32[]{:S(2)}) async-start(bf16[64,16,256]{2,1,0:T(8,128)(2,1)} %shard_map.77), calls=%async_computation | async-start | bytes 1048576 | tf_op jit(solution)/shard_map/all_to_all | solution.py:249
  19.5 0.8 %copy-start.3 = (bf16[64,256]{1,0:T(8,128)(2,1)S(1)}, bf16[64,256]{1,0:T(8,128)(2,1)}, u32[]{:S(2)}) copy-start(bf16[64,256]{1,0:T(8,128)(2,1)} %param.9) | copy-start | bytes 98308
  32.9 0.7 %copy-start = (s32[1024]{0:T(1024)S(1)}, s32[1024]{0:T(1024)}, u32[]{:S(2)}) copy-start(s32[1024]{0:T(1024)} %param.11) | copy-start | bytes 12292
  33.0 0.7 %copy-start.1 = (s32[16]{0:T(128)S(1)}, s32[16]{0:T(128)}, u32[]{:S(2)}) copy-start(s32[16]{0:T(128)} %len_ref.1) | copy-start | bytes 196
  36.7 18.7 %collective-permute-start = (bf16[256,256]{1,0:T(8,128)(2,1)S(1)}, bf16[256,256]{1,0:T(8,128)(2,1)S(1)}, u32[]{:S(2)}, u32[]{:S(2)}) collective-permute-start(bf16[256,256]{1,0:T(8,128)(2,1)S(1)} %pad_maximum_fusion.1), channel_id=1, source_target_pairs={{0,2},{1,3},{2,0},{3,1},{4,6},{5,7},{6,4},{7,5},{8,10},{9,11},{10,... | collective-permute-start | bytes 393224 | tf_op jit(solution)/shard_map/ppermute | solution.py:277
  42.3 13.1 %collective-permute-start.2 = (bf16[128,256]{1,0:T(8,128)(2,1)S(1)}, bf16[128,256]{1,0:T(8,128)(2,1)S(1)}, u32[]{:S(2)}, u32[]{:S(2)}) collective-permute-start(bf16[128,256]{1,0:T(8,128)(2,1)S(1)} %get-tuple-element.27), channel_id=1, source_target_pairs={{0,34},{1,35},{2,32},{3,33},{4,38},{5,39},{6,36},{7,37},{8,42},{9,... | collective-permute-start | bytes 196616 | tf_op jit(solution)/shard_map/ppermute | solution.py:292
  46.0 9.4 %collective-permute-start.1 = (bf16[128,256]{1,0:T(8,128)(2,1)S(1)}, bf16[128,256]{1,0:T(8,128)(2,1)S(1)}, u32[]{:S(2)}, u32[]{:S(2)}) collective-permute-start(bf16[128,256]{1,0:T(8,128)(2,1)S(1)} %get-tuple-element.27), channel_id=1, source_target_pairs={{0,32},{64,96},{128,160},{192,224},{256,288},{320,352},{384,416},{... | collective-permute-start | bytes 196616 | tf_op jit(solution)/shard_map/ppermute | solution.py:291
  48.0 14.5 %all-to-all-start.1 = ((bf16[8,80,256]{2,1,0:T(8,128)(2,1)}), bf16[8,80,256]{2,1,0:T(8,128)(2,1)S(1)}, u32[]{:S(2)}, u32[]{:S(2)}) async-start(bf16[8,80,256]{2,1,0:T(8,128)(2,1)} %shard_map.79), calls=%async_computation.1 | async-start | bytes 655360 | tf_op jit(solution)/shard_map/all_to_all | solution.py:313
  55.4 2.3 %copy-start.2 = (bf16[512,256]{1,0:T(8,128)(2,1)S(1)}, bf16[512,256]{1,0:T(8,128)(2,1)}, u32[]{:S(2)}) copy-start(bf16[512,256]{1,0:T(8,128)(2,1)} %q_ref.1) | copy-start | bytes 786436

commit v6 on v5

--- a/solution.py
+++ b/solution.py
@@ -17,7 +17,7 @@
 QN_DEV = 64
 ROWS = 512
 SHARE = KVH * BLK_DEV
-STAT = 16
+STAT = 8
 
 FAR_BLOCKS = ((0, 0, 128), (0, 128, 256), (0, 384, 128), (1, 0, 256), (1, 256, 128), (1, 384, 128))
 CTX_ROWS = 128

time: 64 us -> 63.7 us (level)
  no operation moved by 1% of the time
where the time goes in v6:
time: 63.7 us; the launch traced here: 63.2 us
  starting transfers between devices  33.3 us (52%)
  blocking collectives  15 us (24%)
  Pallas kernels  8.25 us (13%)
  waiting for transfers between devices  4.32 us (7%)
  local copies, waits for them, and re-layouts  1.4 us (2%)
  between operations  0.8 us (1%)
    all_to_all x1, starting transfers between devices, per_device(): share = lax.all_to_all(send, both, 0, 0, axis_index_groups=plane)  17.1 us
    all_gather x1, blocking collectives, per_device(): lax.all_gather(couple, 'dev', axis=0, tiled=True, axis_index_groups=four)  7.42 us
    all_to_all x1, starting transfers between devices, per_device(): arrived = lax.all_to_all(partial, both, 0, 0, axis_index_groups=line)  7.38 us
    all_gather x1, blocking collectives, per_device(): lax.all_gather(query, 'hst', axis=0, tiled=True, axis_index_groups=pairs)  5.23 us
    ppermute x1, starting transfers between devices, per_device(): lax.ppermute(anchor, both, [(i * len(lanes) + j, (i + 1) * len(lanes) + (...  3.72 us
    ppermute x1, starting transfers between devices, per_device(): flip = lax.ppermute(mine, 'dev', [(i, i ^ 2) for i in lanes])  3.12 us
    pallas_call x1, Pallas kernels, per_device(): pl.pallas_call(far_kernel, out_shape=shape(piece, BF), in_specs=[vmem, vm...  2.48 us
    pallas_call x1, Pallas kernels, per_device(): pl.pallas_call(ctx_kernel, out_shape=shape(ctx_query.shape, BF), in_specs...  2.41 us
  transfers between devices with their start and end apart: 5, of which 2 were waited for; matrix products, arithmetic and copies ran while one was open for 0% of the time, Pallas kernels for 9%

profile of v6, /device:TPU:1, one launch (start us, length us, event | category | flops | bytes accessed | tf_op | source)
XLA Modules:
  0.0 63.2 jit_solution(10609018310352813700)
XLA Ops:
  0.6 1.7 %shard_map.77 = bf16[64,16,256]{2,1,0:T(8,128)(2,1)} custom-call(bf16[16,1024]{1,0:T(8,128)(2,1)} %key_hbm.1, bf16[16,1024]{1,0:T(8,128)(2,1)} %value_hbm.1), custom_call_target="tpu_custom_call" | custom-call | tf_op jit(solution)/shard_map/pallas_call | solution.py:237
  2.3 17.1 %all-to-all-start = ((bf16[64,16,256]{2,1,0:T(8,128)(2,1)}), bf16[64,16,256]{2,1,0:T(8,128)(2,1)S(1)}, u32[]{:S(2)}, u32[]{:S(2)}) async-start(bf16[64,16,256]{2,1,0:T(8,128)(2,1)} %shard_map.77), calls=%async_computation | async-start | bytes 1048576 | tf_op jit(solution)/shard_map/all_to_all | solution.py:249
  19.5 0.0 copy-start.3
  19.5 0.7 %copy-done.3 = bf16[64,256]{1,0:T(8,128)(2,1)S(1)} copy-done((bf16[64,256]{1,0:T(8,128)(2,1)S(1)}, bf16[64,256]{1,0:T(8,128)(2,1)}, u32[]{:S(2)}) %copy-start.3) | copy-done | bytes 32792
  20.2 5.2 %all_gather.9 = bf16[128,256]{1,0:T(8,128)(2,1)S(1)} all-gather(bf16[64,256]{1,0:T(8,128)(2,1)S(1)} %copy-done.3), channel_id=1, replica_groups={{0,32},{64,96},{128,160},{192,224},{256,288},{320,352},{384,416},{448,4..., dimensions={0}, use_global_device_ids=true | all-gather | bytes 98304 | tf_op jit(solution)/shard_map/all_gather | solution.py:252
  25.5 7.4 %all_gather.10.seen_ref = bf16[512,256]{1,0:T(8,128)(2,1)S(1)} all-gather(bf16[128,256]{1,0:T(8,128)(2,1)S(1)} %all_gather.9), channel_id=1, replica_groups={{0,1,2,3},{4,5,6,7},{8,9,10,11},{12,13,14,15},{16,17,18,19},{20,21,22,2..., dimensions={0}, use_global_device_ids=true | all-gather | bytes 327680 | tf_op jit(solution)/shard_map/all_gather | solution.py:253
  32.9 0.0 copy-start
  32.9 0.1 pad_add_fusion.place_ref
  33.0 0.0 copy-start.1
  33.0 0.6 copy-done
  33.6 0.0 copy-done.1
  33.6 0.7 %shard_map.78 = (bf16[2,512,128]{2,1,0:T(8,128)(2,1)S(1)}, f32[8,1024]{1,0:T(8,128)S(1)}, f32[128,128]{1,0:T(8,128)S(1)}, f32[8,512]{1,0:T(8,128)S(1)}, f32[8,128]{1,0:T(8,128)S(1)}) custom-call(bf16[512,256]{1,0:T(8,128)(2,1)S(1)} %all_gather.10.seen_ref, s32[8,128]{1,0:T(8,128)S(1)} %bitcast.8, s32[16]{0:T(128)S(1)} %copy-done.1, s32[4]{0:T(128)S(1)} %pad_add_fusion.place_ref), custom_call_target="tpu_custom_call" | custom-call | tf_op jit(solution)/shard_map/pallas_call | solution.py:256
  34.3 2.3 %all-to-all-done = bf16[64,16,256]{2,1,0:T(8,128)(2,1)S(1)} async-done(((bf16[64,16,256]{2,1,0:T(8,128)(2,1)}), bf16[64,16,256]{2,1,0:T(8,128)(2,1)S(1)}, u32[]{:S(2)}, u32[]{:S(2)}) %all-to-all-start) | async-done | bytes 524320 | tf_op jit(solution)/shard_map/all_to_all | solution.py:249
  36.7 3.1 %collective-permute-start = (bf16[256,256]{1,0:T(8,128)(2,1)S(1)}, bf16[256,256]{1,0:T(8,128)(2,1)S(1)}, u32[]{:S(2)}, u32[]{:S(2)}) collective-permute-start(bf16[256,256]{1,0:T(8,128)(2,1)S(1)} %pad_maximum_fusion.1), channel_id=1, source_target_pairs={{0,2},{1,3},{2,0},{3,1},{4,6},{5,7},{6,4},{7,5},{8,10},{9,11},{10,... | collective-permute-start | bytes 393224 | tf_op jit(solution)/shard_map/ppermute | solution.py:277
  39.8 2.5 %shard_map.79 = bf16[8,72,256]{2,1,0:T(8,128)(2,1)} custom-call(bf16[2,512,128]{2,1,0:T(8,128)(2,1)S(1)} %get-tuple-element.24.q_ref, bf16[1024,256]{1,0:T(8,128)(2,1)S(1)} %bitcast.6, f32[8,1024]{1,0:T(8,128)S(1)} %get-tuple-element.25.spot_ref, f32[128,128]{1,0:T(8,128)S(1)} %get-tuple-element.26.lim_ref), custom_call_target="tpu_custom_call" | custom-call | flops 800000000 | bytes 1200000 | tf_op jit(solution)/shard_map/pallas_call | solution.py:281
  42.3 3.7 %collective-permute-start.2 = (bf16[128,256]{1,0:T(8,128)(2,1)S(1)}, bf16[128,256]{1,0:T(8,128)(2,1)S(1)}, u32[]{:S(2)}, u32[]{:S(2)}) collective-permute-start(bf16[128,256]{1,0:T(8,128)(2,1)S(1)} %get-tuple-element.27), channel_id=1, source_target_pairs={{0,34},{1,35},{2,32},{3,33},{4,38},{5,39},{6,36},{7,37},{8,42},{9,... | collective-permute-start | bytes 196616 | tf_op jit(solution)/shard_map/ppermute | solution.py:292
  46.0 1.9 %collective-permute-start.1 = (bf16[128,256]{1,0:T(8,128)(2,1)S(1)}, bf16[128,256]{1,0:T(8,128)(2,1)S(1)}, u32[]{:S(2)}, u32[]{:S(2)}) collective-permute-start(bf16[128,256]{1,0:T(8,128)(2,1)S(1)} %get-tuple-element.27), channel_id=1, source_target_pairs={{0,32},{64,96},{128,160},{192,224},{256,288},{320,352},{384,416},{... | collective-permute-start | bytes 196616 | tf_op jit(solution)/shard_map/ppermute | solution.py:291
  48.0 7.4 %all-to-all-start.1 = ((bf16[8,72,256]{2,1,0:T(8,128)(2,1)}), bf16[8,72,256]{2,1,0:T(8,128)(2,1)S(1)}, u32[]{:S(2)}, u32[]{:S(2)}) async-start(bf16[8,72,256]{2,1,0:T(8,128)(2,1)} %shard_map.79), calls=%async_computation.1 | async-start | bytes 589824 | tf_op jit(solution)/shard_map/all_to_all | solution.py:313
  55.3 0.0 collective-permute-done.2
  55.3 0.0 collective-permute-done.1
  55.4 0.0 collective-permute-done
  55.4 0.0 copy-start.2
  55.4 2.3 %all_gather.11.kv_ref = bf16[1024,256]{1,0:T(8,128)(2,1)S(1)} all-gather(bf16[512,256]{1,0:T(8,128)(2,1)S(1)} %pad_maximum_fusion), channel_id=1, replica_groups={{0,1},{2,3},{4,5},{6,7},{8,9},{10,11},{12,13},{14,15},{16,17},{18,19},{..., dimensions={0}, use_global_device_ids=true | all-gather | bytes 786432 | tf_op jit(solution)/shard_map/all_gather | solution.py:301
  57.8 0.0 copy-done.2
  57.8 2.4 %shard_map.80 = bf16[512,256]{1,0:T(8,128)(2,1)} custom-call(bf16[512,256]{1,0:T(8,128)(2,1)S(1)} %copy-done.2, bf16[1024,256]{1,0:T(8,128)(2,1)S(1)} %all_gather.11.kv_ref, f32[8,512]{1,0:T(8,128)S(1)} %get-tuple-element.31.own_ref, f32[8,128]{1,0:T(8,128)S(1)} %get-tuple-element.32.gate_ref), custom_call_target="tpu_custom_call" | custom-call | flops 800000000 | bytes 1200000 | tf_op jit(solution)/shard_map/pallas_call | solution.py:315
  60.2 2.0 %all-to-all-done.1.in_ref = bf16[8,72,256]{2,1,0:T(8,128)(2,1)S(1)} async-done(((bf16[8,72,256]{2,1,0:T(8,128)(2,1)}), bf16[8,72,256]{2,1,0:T(8,128)(2,1)S(1)}, u32[]{:S(2)}, u32[]{:S(2)}) %all-to-all-start.1) | async-done | bytes 294944 | tf_op jit(solution)/shard_map/all_to_all | solution.py:313
  62.2 1.0 %shard_map.81 = bf16[64,256]{1,0:T(8,128)(2,1)} custom-call(bf16[8,72,256]{2,1,0:T(8,128)(2,1)S(1)} %all-to-all-done.1.in_ref), custom_call_target="tpu_custom_call" | custom-call | tf_op jit(solution)/shard_map/pallas_call | solution.py:328
  (4 shorter events, 0.1 us)
Async XLA Ops:
  2.3 34.3 %all-to-all-start = ((bf16[64,16,256]{2,1,0:T(8,128)(2,1)}), bf16[64,16,256]{2,1,0:T(8,128)(2,1)S(1)}, u32[]{:S(2)}, u32[]{:S(2)}) async-start(bf16[64,16,256]{2,1,0:T(8,128)(2,1)} %shard_map.77), calls=%async_computation | async-start | bytes 1048576 | tf_op jit(solution)/shard_map/all_to_all | solution.py:249
  19.5 0.8 %copy-start.3 = (bf16[64,256]{1,0:T(8,128)(2,1)S(1)}, bf16[64,256]{1,0:T(8,128)(2,1)}, u32[]{:S(2)}) copy-start(bf16[64,256]{1,0:T(8,128)(2,1)} %param.9) | copy-start | bytes 98308
  32.9 0.7 %copy-start = (s32[1024]{0:T(1024)S(1)}, s32[1024]{0:T(1024)}, u32[]{:S(2)}) copy-start(s32[1024]{0:T(1024)} %param.11) | copy-start | bytes 12292
  33.0 0.7 %copy-start.1 = (s32[16]{0:T(128)S(1)}, s32[16]{0:T(128)}, u32[]{:S(2)}) copy-start(s32[16]{0:T(128)} %len_ref.1) | copy-start | bytes 196
  36.7 18.7 %collective-permute-start = (bf16[256,256]{1,0:T(8,128)(2,1)S(1)}, bf16[256,256]{1,0:T(8,128)(2,1)S(1)}, u32[]{:S(2)}, u32[]{:S(2)}) collective-permute-start(bf16[256,256]{1,0:T(8,128)(2,1)S(1)} %pad_maximum_fusion.1), channel_id=1, source_target_pairs={{0,2},{1,3},{2,0},{3,1},{4,6},{5,7},{6,4},{7,5},{8,10},{9,11},{10,... | collective-permute-start | bytes 393224 | tf_op jit(solution)/shard_map/ppermute | solution.py:277
  42.3 13.1 %collective-permute-start.2 = (bf16[128,256]{1,0:T(8,128)(2,1)S(1)}, bf16[128,256]{1,0:T(8,128)(2,1)S(1)}, u32[]{:S(2)}, u32[]{:S(2)}) collective-permute-start(bf16[128,256]{1,0:T(8,128)(2,1)S(1)} %get-tuple-element.27), channel_id=1, source_target_pairs={{0,34},{1,35},{2,32},{3,33},{4,38},{5,39},{6,36},{7,37},{8,42},{9,... | collective-permute-start | bytes 196616 | tf_op jit(solution)/shard_map/ppermute | solution.py:292
  46.0 9.3 %collective-permute-start.1 = (bf16[128,256]{1,0:T(8,128)(2,1)S(1)}, bf16[128,256]{1,0:T(8,128)(2,1)S(1)}, u32[]{:S(2)}, u32[]{:S(2)}) collective-permute-start(bf16[128,256]{1,0:T(8,128)(2,1)S(1)} %get-tuple-element.27), channel_id=1, source_target_pairs={{0,32},{64,96},{128,160},{192,224},{256,288},{320,352},{384,416},{... | collective-permute-start | bytes 196616 | tf_op jit(solution)/shard_map/ppermute | solution.py:291
  48.0 14.2 %all-to-all-start.1 = ((bf16[8,72,256]{2,1,0:T(8,128)(2,1)}), bf16[8,72,256]{2,1,0:T(8,128)(2,1)S(1)}, u32[]{:S(2)}, u32[]{:S(2)}) async-start(bf16[8,72,256]{2,1,0:T(8,128)(2,1)} %shard_map.79), calls=%async_computation.1 | async-start | bytes 589824 | tf_op jit(solution)/shard_map/all_to_all | solution.py:313
  55.4 2.3 %copy-start.2 = (bf16[512,256]{1,0:T(8,128)(2,1)S(1)}, bf16[512,256]{1,0:T(8,128)(2,1)}, u32[]{:S(2)}) copy-start(bf16[512,256]{1,0:T(8,128)(2,1)} %q_ref.1) | copy-start | bytes 786436

commit v7 on v5

--- a/solution.py
+++ b/solution.py
@@ -19,7 +19,7 @@
 SHARE = KVH * BLK_DEV
 STAT = 16
 
-FAR_BLOCKS = ((0, 0, 128), (0, 128, 256), (0, 384, 128), (1, 0, 256), (1, 256, 128), (1, 384, 128))
+FAR_BLOCKS = ((0, 0, 256), (0, 256, 256), (1, 0, 256), (1, 256, 128), (1, 384, 128))
 CTX_ROWS = 128
 NEG = -1e30
 FAR = 1 << 20

time: 64 us -> 64 us (level)
  no operation moved by 1% of the time
where the time goes in v7:
time: 64 us; the launch traced here: 63.5 us
  starting transfers between devices  33.3 us (52%)
  blocking collectives  15 us (23%)
  Pallas kernels  8.23 us (13%)
  waiting for transfers between devices  4.63 us (7%)
  local copies, waits for them, and re-layouts  1.4 us (2%)
  between operations  0.8 us (1%)
    all_to_all x1, starting transfers between devices, per_device(): share = lax.all_to_all(send, both, 0, 0, axis_index_groups=plane)  17.1 us
    all_gather x1, blocking collectives, per_device(): lax.all_gather(couple, 'dev', axis=0, tiled=True, axis_index_groups=four)  7.42 us
    all_to_all x1, starting transfers between devices, per_device(): arrived = lax.all_to_all(partial, both, 0, 0, axis_index_groups=line)  7.4 us
    all_gather x1, blocking collectives, per_device(): lax.all_gather(query, 'hst', axis=0, tiled=True, axis_index_groups=pairs)  5.23 us
    ppermute x1, starting transfers between devices, per_device(): lax.ppermute(anchor, both, [(i * len(lanes) + j, (i + 1) * len(lanes) + (...  3.72 us
    ppermute x1, starting transfers between devices, per_device(): flip = lax.ppermute(mine, 'dev', [(i, i ^ 2) for i in lanes])  3.12 us
    pallas_call x1, Pallas kernels, per_device(): pl.pallas_call(far_kernel, out_shape=shape(piece, BF), in_specs=[vmem, vm...  2.46 us
    pallas_call x1, Pallas kernels, per_device(): pl.pallas_call(ctx_kernel, out_shape=shape(ctx_query.shape, BF), in_specs...  2.41 us
  transfers between devices with their start and end apart: 5, of which 2 were waited for; matrix products, arithmetic and copies ran while one was open for 0% of the time, Pallas kernels for 9%

profile of v7, /device:TPU:1, one launch (start us, length us, event | category | flops | bytes accessed | tf_op | source)
XLA Modules:
  0.0 63.5 jit_solution(9851948696414835373)
XLA Ops:
  0.6 1.7 %shard_map.77 = bf16[64,16,256]{2,1,0:T(8,128)(2,1)} custom-call(bf16[16,1024]{1,0:T(8,128)(2,1)} %key_hbm.1, bf16[16,1024]{1,0:T(8,128)(2,1)} %value_hbm.1), custom_call_target="tpu_custom_call" | custom-call | tf_op jit(solution)/shard_map/pallas_call | solution.py:237
  2.3 17.1 %all-to-all-start = ((bf16[64,16,256]{2,1,0:T(8,128)(2,1)}), bf16[64,16,256]{2,1,0:T(8,128)(2,1)S(1)}, u32[]{:S(2)}, u32[]{:S(2)}) async-start(bf16[64,16,256]{2,1,0:T(8,128)(2,1)} %shard_map.77), calls=%async_computation | async-start | bytes 1048576 | tf_op jit(solution)/shard_map/all_to_all | solution.py:249
  19.5 0.0 copy-start.3
  19.5 0.7 %copy-done.3 = bf16[64,256]{1,0:T(8,128)(2,1)S(1)} copy-done((bf16[64,256]{1,0:T(8,128)(2,1)S(1)}, bf16[64,256]{1,0:T(8,128)(2,1)}, u32[]{:S(2)}) %copy-start.3) | copy-done | bytes 32792
  20.2 5.2 %all_gather.9 = bf16[128,256]{1,0:T(8,128)(2,1)S(1)} all-gather(bf16[64,256]{1,0:T(8,128)(2,1)S(1)} %copy-done.3), channel_id=1, replica_groups={{0,32},{64,96},{128,160},{192,224},{256,288},{320,352},{384,416},{448,4..., dimensions={0}, use_global_device_ids=true | all-gather | bytes 98304 | tf_op jit(solution)/shard_map/all_gather | solution.py:252
  25.5 7.4 %all_gather.10.seen_ref = bf16[512,256]{1,0:T(8,128)(2,1)S(1)} all-gather(bf16[128,256]{1,0:T(8,128)(2,1)S(1)} %all_gather.9), channel_id=1, replica_groups={{0,1,2,3},{4,5,6,7},{8,9,10,11},{12,13,14,15},{16,17,18,19},{20,21,22,2..., dimensions={0}, use_global_device_ids=true | all-gather | bytes 327680 | tf_op jit(solution)/shard_map/all_gather | solution.py:253
  32.9 0.0 copy-start
  32.9 0.1 pad_add_fusion.place_ref
  33.0 0.0 copy-start.1
  33.0 0.6 copy-done
  33.6 0.0 copy-done.1
  33.6 0.7 %shard_map.78 = (bf16[2,512,128]{2,1,0:T(8,128)(2,1)S(1)}, f32[8,1024]{1,0:T(8,128)S(1)}, f32[128,128]{1,0:T(8,128)S(1)}, f32[8,512]{1,0:T(8,128)S(1)}, f32[8,128]{1,0:T(8,128)S(1)}) custom-call(bf16[512,256]{1,0:T(8,128)(2,1)S(1)} %all_gather.10.seen_ref, s32[8,128]{1,0:T(8,128)S(1)} %bitcast.8, s32[16]{0:T(128)S(1)} %copy-done.1, s32[4]{0:T(128)S(1)} %pad_add_fusion.place_ref), custom_call_target="tpu_custom_call" | custom-call | tf_op jit(solution)/shard_map/pallas_call | solution.py:256
  34.3 2.3 %all-to-all-done = bf16[64,16,256]{2,1,0:T(8,128)(2,1)S(1)} async-done(((bf16[64,16,256]{2,1,0:T(8,128)(2,1)}), bf16[64,16,256]{2,1,0:T(8,128)(2,1)S(1)}, u32[]{:S(2)}, u32[]{:S(2)}) %all-to-all-start) | async-done | bytes 524320 | tf_op jit(solution)/shard_map/all_to_all | solution.py:249
  36.7 3.1 %collective-permute-start = (bf16[256,256]{1,0:T(8,128)(2,1)S(1)}, bf16[256,256]{1,0:T(8,128)(2,1)S(1)}, u32[]{:S(2)}, u32[]{:S(2)}) collective-permute-start(bf16[256,256]{1,0:T(8,128)(2,1)S(1)} %pad_maximum_fusion.1), channel_id=1, source_target_pairs={{0,2},{1,3},{2,0},{3,1},{4,6},{5,7},{6,4},{7,5},{8,10},{9,11},{10,... | collective-permute-start | bytes 393224 | tf_op jit(solution)/shard_map/ppermute | solution.py:277
  39.8 2.5 %shard_map.79 = bf16[8,80,256]{2,1,0:T(8,128)(2,1)} custom-call(bf16[2,512,128]{2,1,0:T(8,128)(2,1)S(1)} %get-tuple-element.24.q_ref, bf16[1024,256]{1,0:T(8,128)(2,1)S(1)} %bitcast.6, f32[8,1024]{1,0:T(8,128)S(1)} %get-tuple-element.25.spot_ref, f32[128,128]{1,0:T(8,128)S(1)} %get-tuple-element.26.lim_ref), custom_call_target="tpu_custom_call" | custom-call | flops 800000000 | bytes 1200000 | tf_op jit(solution)/shard_map/pallas_call | solution.py:281
  42.3 3.7 %collective-permute-start.2 = (bf16[128,256]{1,0:T(8,128)(2,1)S(1)}, bf16[128,256]{1,0:T(8,128)(2,1)S(1)}, u32[]{:S(2)}, u32[]{:S(2)}) collective-permute-start(bf16[128,256]{1,0:T(8,128)(2,1)S(1)} %get-tuple-element.27), channel_id=1, source_target_pairs={{0,34},{1,35},{2,32},{3,33},{4,38},{5,39},{6,36},{7,37},{8,42},{9,... | collective-permute-start | bytes 196616 | tf_op jit(solution)/shard_map/ppermute | solution.py:292
  46.0 1.9 %collective-permute-start.1 = (bf16[128,256]{1,0:T(8,128)(2,1)S(1)}, bf16[128,256]{1,0:T(8,128)(2,1)S(1)}, u32[]{:S(2)}, u32[]{:S(2)}) collective-permute-start(bf16[128,256]{1,0:T(8,128)(2,1)S(1)} %get-tuple-element.27), channel_id=1, source_target_pairs={{0,32},{64,96},{128,160},{192,224},{256,288},{320,352},{384,416},{... | collective-permute-start | bytes 196616 | tf_op jit(solution)/shard_map/ppermute | solution.py:291
  47.9 7.4 %all-to-all-start.1 = ((bf16[8,80,256]{2,1,0:T(8,128)(2,1)}), bf16[8,80,256]{2,1,0:T(8,128)(2,1)S(1)}, u32[]{:S(2)}, u32[]{:S(2)}) async-start(bf16[8,80,256]{2,1,0:T(8,128)(2,1)} %shard_map.79), calls=%async_computation.1 | async-start | bytes 655360 | tf_op jit(solution)/shard_map/all_to_all | solution.py:313
  55.3 0.0 collective-permute-done.2
  55.3 0.0 collective-permute-done.1
  55.3 0.0 collective-permute-done
  55.4 0.0 copy-start.2
  55.4 2.3 %all_gather.11.kv_ref = bf16[1024,256]{1,0:T(8,128)(2,1)S(1)} all-gather(bf16[512,256]{1,0:T(8,128)(2,1)S(1)} %pad_maximum_fusion), channel_id=1, replica_groups={{0,1},{2,3},{4,5},{6,7},{8,9},{10,11},{12,13},{14,15},{16,17},{18,19},{..., dimensions={0}, use_global_device_ids=true | all-gather | bytes 786432 | tf_op jit(solution)/shard_map/all_gather | solution.py:301
  57.7 0.0 copy-done.2
  57.8 2.4 %shard_map.80 = bf16[512,256]{1,0:T(8,128)(2,1)} custom-call(bf16[512,256]{1,0:T(8,128)(2,1)S(1)} %copy-done.2, bf16[1024,256]{1,0:T(8,128)(2,1)S(1)} %all_gather.11.kv_ref, f32[8,512]{1,0:T(8,128)S(1)} %get-tuple-element.31.own_ref, f32[8,128]{1,0:T(8,128)S(1)} %get-tuple-element.32.gate_ref), custom_call_target="tpu_custom_call" | custom-call | flops 800000000 | bytes 1200000 | tf_op jit(solution)/shard_map/pallas_call | solution.py:315
  60.2 2.3 %all-to-all-done.1.in_ref = bf16[8,80,256]{2,1,0:T(8,128)(2,1)S(1)} async-done(((bf16[8,80,256]{2,1,0:T(8,128)(2,1)}), bf16[8,80,256]{2,1,0:T(8,128)(2,1)S(1)}, u32[]{:S(2)}, u32[]{:S(2)}) %all-to-all-start.1) | async-done | bytes 327712 | tf_op jit(solution)/shard_map/all_to_all | solution.py:313
  62.5 1.0 %shard_map.81 = bf16[64,256]{1,0:T(8,128)(2,1)} custom-call(bf16[8,80,256]{2,1,0:T(8,128)(2,1)S(1)} %all-to-all-done.1.in_ref), custom_call_target="tpu_custom_call" | custom-call | tf_op jit(solution)/shard_map/pallas_call | solution.py:328
  (4 shorter events, 0.1 us)
Async XLA Ops:
  2.3 34.3 %all-to-all-start = ((bf16[64,16,256]{2,1,0:T(8,128)(2,1)}), bf16[64,16,256]{2,1,0:T(8,128)(2,1)S(1)}, u32[]{:S(2)}, u32[]{:S(2)}) async-start(bf16[64,16,256]{2,1,0:T(8,128)(2,1)} %shard_map.77), calls=%async_computation | async-start | bytes 1048576 | tf_op jit(solution)/shard_map/all_to_all | solution.py:249
  19.5 0.8 %copy-start.3 = (bf16[64,256]{1,0:T(8,128)(2,1)S(1)}, bf16[64,256]{1,0:T(8,128)(2,1)}, u32[]{:S(2)}) copy-start(bf16[64,256]{1,0:T(8,128)(2,1)} %param.9) | copy-start | bytes 98308
  32.9 0.7 %copy-start = (s32[1024]{0:T(1024)S(1)}, s32[1024]{0:T(1024)}, u32[]{:S(2)}) copy-start(s32[1024]{0:T(1024)} %param.11) | copy-start | bytes 12292
  33.0 0.7 %copy-start.1 = (s32[16]{0:T(128)S(1)}, s32[16]{0:T(128)}, u32[]{:S(2)}) copy-start(s32[16]{0:T(128)} %len_ref.1) | copy-start | bytes 196
  36.7 18.7 %collective-permute-start = (bf16[256,256]{1,0:T(8,128)(2,1)S(1)}, bf16[256,256]{1,0:T(8,128)(2,1)S(1)}, u32[]{:S(2)}, u32[]{:S(2)}) collective-permute-start(bf16[256,256]{1,0:T(8,128)(2,1)S(1)} %pad_maximum_fusion.1), channel_id=1, source_target_pairs={{0,2},{1,3},{2,0},{3,1},{4,6},{5,7},{6,4},{7,5},{8,10},{9,11},{10,... | collective-permute-start | bytes 393224 | tf_op jit(solution)/shard_map/ppermute | solution.py:277
  42.3 13.1 %collective-permute-start.2 = (bf16[128,256]{1,0:T(8,128)(2,1)S(1)}, bf16[128,256]{1,0:T(8,128)(2,1)S(1)}, u32[]{:S(2)}, u32[]{:S(2)}) collective-permute-start(bf16[128,256]{1,0:T(8,128)(2,1)S(1)} %get-tuple-element.27), channel_id=1, source_target_pairs={{0,34},{1,35},{2,32},{3,33},{4,38},{5,39},{6,36},{7,37},{8,42},{9,... | collective-permute-start | bytes 196616 | tf_op jit(solution)/shard_map/ppermute | solution.py:292
  46.0 9.4 %collective-permute-start.1 = (bf16[128,256]{1,0:T(8,128)(2,1)S(1)}, bf16[128,256]{1,0:T(8,128)(2,1)S(1)}, u32[]{:S(2)}, u32[]{:S(2)}) collective-permute-start(bf16[128,256]{1,0:T(8,128)(2,1)S(1)} %get-tuple-element.27), channel_id=1, source_target_pairs={{0,32},{64,96},{128,160},{192,224},{256,288},{320,352},{384,416},{... | collective-permute-start | bytes 196616 | tf_op jit(solution)/shard_map/ppermute | solution.py:291
  47.9 14.5 %all-to-all-start.1 = ((bf16[8,80,256]{2,1,0:T(8,128)(2,1)}), bf16[8,80,256]{2,1,0:T(8,128)(2,1)S(1)}, u32[]{:S(2)}, u32[]{:S(2)}) async-start(bf16[8,80,256]{2,1,0:T(8,128)(2,1)} %shard_map.79), calls=%async_computation.1 | async-start | bytes 655360 | tf_op jit(solution)/shard_map/all_to_all | solution.py:313
  55.4 2.3 %copy-start.2 = (bf16[512,256]{1,0:T(8,128)(2,1)S(1)}, bf16[512,256]{1,0:T(8,128)(2,1)}, u32[]{:S(2)}) copy-start(bf16[512,256]{1,0:T(8,128)(2,1)} %q_ref.1) | copy-start | bytes 786436
